TPU v7x, 512 devices: a whole 4x4x16 slice. The times are simulated.
512 devices in a mesh: leaf: 32 (over z, core), vec: 16 (over y, x).
Axes of the slice: x: 4, y: 4, z: 16, core: 2. Of those that a mesh axis runs over, the one named last changes fastest.
Arguments:
- points: bfloat16 [512, 3, 256], P('leaf'), may hold values from 0 to 1
- probe_vectors: bfloat16 [512, 256, 256], P('leaf', 'vec'), may hold values from -6 to 6
- neighbours: int32 [512, 16], P('leaf'), may hold values from -1 to 511, as said below
- leaf_pivots: int32 [512, 64], P('leaf'), may hold values from 0 to 255, as said below
- leaf_inverse: float32 [512, 64, 64], P('leaf'), as said below
- local_pivots: int32 [480, 64], P('leaf'), may hold values from 0 to 127, as said below
- local_inverse: float32 [480, 64, 64], P('leaf'), as said below
- upper_pivots: int32 [28, 64], replicated, may hold values from 0 to 127, as said below
- upper_inverse: float32 [28, 64, 64], replicated, as said below
Outputs:
- leaf_interp: float32 [512, 256, 64], P('leaf')
- local_interp: float32 [480, 128, 64], P('leaf')
- upper_interp: float32 [32, 3, 128, 64], P('leaf')
- top_sketch: float32 [32, 256, 64], P('leaf', 'vec')
Inputs may be any that keep to these rules, and one draw needn't show every extreme that they name: Entry 0 of neighbours[i] is i; then come distinct clusters j != i with |j - i| <= 16, then -1 to the end. The first cluster of each group of 16 lists the cluster before it in entry 1, and the last one lists the cluster after it there, where those exist. A list holds at least 4 clusters, and some lists hold 16. `leaf_pivots`: each row holds 64 distinct row numbers. `local_pivots`: each row holds 64 distinct row numbers. `upper_pivots`: each row holds 64 distinct row numbers. `leaf_inverse`: diagonal entries lie in 0.5 to 1.5. `local_inverse`: diagonal entries lie in 0.5 to 1.5. `upper_inverse`: diagonal entries lie in 0.5 to 1.5.
All inputs are finite; a program needn't handle non-finite values.
Results may differ from a plain program's by a relative error of at most 0.0013.
Values may be sent and summed in bfloat16 or wider, within the bound.
A program may use at most 64 MiB of HBM per device.

v0:
```python
import jax
import jax.numpy as jnp
from jax import lax
from jax.sharding import PartitionSpec as P

UPL = 3


SOFTEN = 0.0009
EPSILON = 1e-06


def padded(shard, sides, width):
    for axis, dim in sides:
        count, length = (lax.axis_size(axis), shard.shape[dim])
        up = [(i, (i + 1) % count) for i in range(count - 1)]
        down = [(j, i) for i, j in up]
        last = lax.slice_in_dim(shard, length - width, length, axis=dim)
        initial = lax.slice_in_dim(shard, 0, width, axis=dim)
        before = lax.ppermute(last, axis, up)
        after = lax.ppermute(initial, axis, down)
        shard = jnp.concatenate([before, shard, after], axis=dim)
    return shard


def shifted(shard, axis, by):
    count = lax.axis_size(axis)
    pairs = [(i, i + by) for i in range(count) if 0 <= i + by < count]
    return lax.ppermute(shard, axis, pairs)


def kernel_tile(near_points, far_points):
    near_xyz = near_points.astype(jnp.float32)
    far_xyz = far_points.astype(jnp.float32)
    distance = SOFTEN + jnp.zeros(
        (near_xyz.shape[0], near_xyz.shape[2], far_xyz.shape[2]), jnp.float32
    )
    for coordinate in range(3):
        offset_gap = near_xyz[:, coordinate, :, None] - far_xyz[:, coordinate, None, :]
        distance = distance + offset_gap * offset_gap
    return 1.0 / (64.0 * jnp.sqrt(distance))


def interpolate(sketch, pivots, inverse, column_total, combine_stats):
    rows = sketch.shape[2]
    index_grid = jnp.broadcast_to(
        pivots[:, None, :], (sketch.shape[0], sketch.shape[1], pivots.shape[1])
    )
    chosen = jnp.take_along_axis(sketch, index_grid, axis=2)
    gram_rows = jnp.einsum("nsp,nsk->npk", sketch, chosen, precision=lax.Precision.HIGHEST)
    squares = jnp.sum(sketch * sketch, axis=(1, 2))
    gram_rows, squares = combine_stats(gram_rows, squares)
    mean_sq = squares / (rows * column_total) + EPSILON
    interp_map = jnp.einsum("npl,nlk->npk", gram_rows, inverse, precision=lax.Precision.HIGHEST)
    interp_map = interp_map / (column_total * mean_sq)[:, None, None]
    upward = jnp.einsum("nsp,npk->nsk", sketch, interp_map, precision=lax.Precision.HIGHEST)
    upward = upward / jnp.sqrt(mean_sq)[:, None, None]
    return (interp_map, upward)


def pair_children(upward):
    node_count = upward.shape[0] // 2
    paired = upward.reshape(node_count, 2, upward.shape[1], upward.shape[2])
    paired = jnp.transpose(paired, (0, 2, 1, 3))
    return paired.reshape(node_count, upward.shape[1], 2 * upward.shape[2])


def on_device(
    points,
    probe_vectors,
    neighbours,
    leaf_pivots,
    leaf_inverse,
    local_pivots,
    local_inverse,
    upper_pivots,
    upper_inverse,
):
    leaf_count = points.shape[0]
    slot_total = neighbours.shape[1]
    columns_here = probe_vectors.shape[1]
    rank_kept = leaf_pivots.shape[1]
    device_index = lax.axis_index("leaf")
    group_total = lax.axis_size("leaf")
    joined = jnp.concatenate([points, probe_vectors], axis=1)
    extended = padded(joined, (("leaf", 0),), leaf_count)
    first_cluster = device_index * leaf_count - leaf_count

    def add_slot(slot_index, running):
        listed = lax.dynamic_slice_in_dim(neighbours, slot_index, 1, 1)[:, 0]
        present = listed >= 0
        position = jnp.clip(listed - first_cluster, 0, 3 * leaf_count - 1)
        blocks = jnp.take(extended, position, axis=0)
        kernel_block = jnp.where(
            present[:, None, None], kernel_tile(points, blocks[:, :3]), 0.0
        ).astype(jnp.bfloat16)
        return running + jnp.einsum(
            "nsq,npq->nsp", blocks[:, 3:], kernel_block, preferred_element_type=jnp.float32
        )

    sketch = lax.fori_loop(
        0, slot_total, add_slot, jnp.zeros((leaf_count, columns_here, points.shape[2]), jnp.float32)
    )
    column_total = columns_here * lax.axis_size("vec")

    def combine_stats(gram_rows, squares):
        return lax.psum((gram_rows, squares), "vec")

    leaf_interp, upward = interpolate(
        sketch, leaf_pivots, leaf_inverse, column_total, combine_stats
    )
    pieces = []
    offset = 0
    while upward.shape[0] > 1:
        node_count = upward.shape[0] // 2
        interp_map, upward = interpolate(
            pair_children(upward),
            local_pivots[offset : offset + node_count],
            local_inverse[offset : offset + node_count],
            column_total,
            combine_stats,
        )
        pieces.append(interp_map)
        offset = offset + node_count
    local_interp = jnp.concatenate(pieces, axis=0)
    own_sketch = upward[0]
    heap_offset = 0
    upper_maps = []
    for tier_index in range(UPL):
        partner = shifted(own_sketch, "leaf", -(1 << tier_index))
        node_index = heap_offset + (device_index >> tier_index + 1)
        interp_map, upward = interpolate(
            jnp.concatenate([own_sketch, partner], axis=1)[None],
            lax.dynamic_slice_in_dim(upper_pivots, node_index, 1, 0),
            lax.dynamic_slice_in_dim(upper_inverse, node_index, 1, 0),
            column_total,
            combine_stats,
        )
        upper_maps.append(interp_map[0])
        own_sketch = upward[0]
        heap_offset = heap_offset + (group_total >> tier_index + 1)
    map_rows = UPL * 2 * rank_kept
    packed = jnp.concatenate(
        [jnp.stack(upper_maps, axis=0).reshape(map_rows, rank_kept), own_sketch], axis=0
    )
    row_number = jnp.arange(packed.shape[0], dtype=jnp.int32)
    row_tier = jnp.minimum(row_number // (2 * rank_kept), UPL)
    for tier_index in reversed(range(UPL)):
        arrived = shifted(packed, "leaf", 1 << tier_index)
        take_rows = (device_index >> tier_index & 1 == 1) & (row_tier >= tier_index)
        packed = jnp.where(take_rows[:, None], arrived, packed)
    stacked = packed[:map_rows].reshape(UPL, 2 * rank_kept, rank_kept)
    own_sketch = packed[map_rows:]
    return (leaf_interp, local_interp, stacked[None], own_sketch[None])


def solution(mesh):
    placed = (
        P("leaf", None, None),
        P("leaf", "vec", None),
        P("leaf", None),
        P("leaf", None),
        P("leaf", None, None),
        P("leaf", None),
        P("leaf", None, None),
        P(),
        P(),
    )
    return jax.shard_map(
        on_device,
        mesh=mesh,
        in_specs=placed,
        out_specs=(
            P("leaf", None, None),
            P("leaf", None, None),
            P("leaf", None, None, None),
            P("leaf", "vec", None),
        ),
        check_vma=False,
    )
```

profile of v0, /device:TPU:1, one launch (start us, length us, event | category | flops | bytes accessed | tf_op | source)
XLA Modules:
  0.0 1230.4 jit_solution(7921179615176254731)
XLA Ops:
  29.3 79.5 %while.14 = (s32[]{:T(128)}, f32[16,16,256]{2,1,0:T(8,128)S(1)}, s32[16,16]{0,1:T(8,128)S(1)}, s32[]{:T(128)}, bf16[48,19,256]{2,1,0:T(8,128)(2,1)S(1)}, /*index...) while((s32[]{:T(128)}, f32[16,16,256]{2,1,0:T(8,128)S(1)}, s32[16,16]{0,1:T(8,128)S(1)}, ...), condition=%wide.region_1.2_spmd.clone, body=%wide.region_0.1_spmd.clone.sunk | while | flops 47420560 | bytes 1823639 | solution.py:101
  108.8 161.0 %gather_fusion.1 = f32[16384]{0:T(1024)S(1)} fusion(f32[16,16,256]{2,1,0:T(8,128)S(1)} %get-tuple-element.114, s32[16384]{0:T(1024)S(1)} %reshape.429), kind=kCustom, calls=%fused_computation.5 | custom fusion | bytes 327680 | tf_op jit(solution)/shard_map/jit(take_along_axis)/gather | solution.py:49
  272.5 30.5 %psum.113 = f32[16]{0:T(128)S(1)} all-reduce(f32[16]{0:T(128)S(1)} %multiply_reduce_fusion), channel_id=1, replica_groups=mesh['leaf'=32,'vec'=16] {'vec'}, use_global_device_ids=true, to_apply=%region_4.5 | all-reduce | flops 16 | bytes 128 | tf_op jit(solution)/shard_map/psum | solution.py:107
  303.0 87.5 %all-reduce.9.cloned.1.call-done = f32[16,256,64]{1,2,0:T(8,128)} async-done(((f32[16,256,64]{1,2,0:T(8,128)}), f32[16,256,64]{1,2,0:T(8,128)}) %all-reduce.9.cloned.1.call-update) | async-done | bytes 1048592 | tf_op jit(solution)/shard_map/psum | solution.py:107
  394.0 65.8 %gather_fusion.2 = f32[8192]{0:T(1024)S(1)} fusion(f32[8,16,128]{2,1,0:T(8,128)S(1)} %reshape.361, s32[8192]{0:T(1024)S(1)} %reshape.435), kind=kCustom, calls=%fused_computation.6 | custom fusion | bytes 163840 | tf_op jit(solution)/shard_map/jit(take_along_axis)/gather | solution.py:49
  461.5 30.9 %psum.115 = f32[8]{0:T(128)S(1)} all-reduce(f32[8]{0:T(128)S(1)} %multiply_reduce_fusion.1), channel_id=1, replica_groups=mesh['leaf'=32,'vec'=16] {'vec'}, use_global_device_ids=true, to_apply=%region_7.8 | all-reduce | flops 8 | bytes 64 | tf_op jit(solution)/shard_map/psum | solution.py:107
  492.4 83.5 %all-reduce.11.cloned.1.call-done = f32[8,128,64]{1,2,0:T(8,128)} async-done(((f32[8,128,64]{1,2,0:T(8,128)}), f32[8,128,64]{1,2,0:T(8,128)}) %all-reduce.11.cloned.1.call-update) | async-done | bytes 262160 | tf_op jit(solution)/shard_map/psum | solution.py:107
  578.3 33.2 %gather_fusion.3 = f32[4096]{0:T(1024)S(1)} fusion(f32[4,16,128]{2,1,0:T(8,128)S(1)} %reshape.363, s32[4096]{0:T(1024)S(1)} %reshape.441), kind=kCustom, calls=%fused_computation.7 | custom fusion | bytes 81920 | tf_op jit(solution)/shard_map/jit(take_along_axis)/gather | solution.py:49
  612.7 31.2 %psum.117 = f32[4]{0:T(128)S(1)} all-reduce(f32[4]{0:T(128)S(1)} %multiply_reduce_fusion.2), channel_id=1, replica_groups=mesh['leaf'=32,'vec'=16] {'vec'}, use_global_device_ids=true, to_apply=%region_10.11 | all-reduce | flops 4 | bytes 32 | tf_op jit(solution)/shard_map/psum | solution.py:107
  643.9 81.1 %all-reduce.13.cloned.1.call-done = f32[4,128,64]{1,2,0:T(8,128)} async-done(((f32[4,128,64]{1,2,0:T(8,128)}), f32[4,128,64]{1,2,0:T(8,128)}) %all-reduce.13.cloned.1.call-update) | async-done | bytes 131088 | tf_op jit(solution)/shard_map/psum | solution.py:107
  726.8 16.9 %gather_fusion.4 = f32[2048]{0:T(1024)S(1)} fusion(f32[2,16,128]{2,1,0:T(8,128)S(1)} %reshape.365, s32[2048]{0:T(1024)S(1)} %reshape.447), kind=kCustom, calls=%fused_computation.8 | custom fusion | bytes 40960 | tf_op jit(solution)/shard_map/jit(take_along_axis)/gather | solution.py:49
  744.7 31.5 %psum.119 = f32[2]{0:T(128)S(1)} all-reduce(f32[2]{0:T(128)S(1)} %multiply_reduce_fusion.3), channel_id=1, replica_groups=mesh['leaf'=32,'vec'=16] {'vec'}, use_global_device_ids=true, to_apply=%region_13.14 | all-reduce | flops 2 | bytes 16 | tf_op jit(solution)/shard_map/psum | solution.py:107
  776.2 79.8 %all-reduce.15.cloned.1.call-done = f32[2,128,64]{1,2,0:T(8,128)} async-done(((f32[2,128,64]{1,2,0:T(8,128)}), f32[2,128,64]{1,2,0:T(8,128)}) %all-reduce.15.cloned.1.call-update) | async-done | bytes 65552 | tf_op jit(solution)/shard_map/psum | solution.py:107
  858.0 6.8 gather_fusion.5
  865.2 60.0 %all-reduce.3 = (f32[128,64]{1,0:T(8,128)S(1)}, f32[1]{0:T(128)}) all-reduce(f32[128,64]{1,0:T(8,128)S(1)} %fusion.75, f32[1]{0:T(128)} %bitcast.16), channel_id=1, replica_groups=mesh['leaf'=32,'vec'=16] {'vec'}, use_global_device_ids=true, to_apply=%region_14.16 | all-reduce | flops 8193 | bytes 65544 | tf_op jit(solution)/shard_map/psum | solution.py:107
  926.3 18.3 %collective-permute-start.2 = (f32[16,64]{1,0:T(8,128)S(1)}, f32[16,64]{1,0:T(8,128)S(1)}, u32[]{:S(2)}, u32[]{:S(2)}) collective-permute-start(f32[16,64]{1,0:T(8,128)S(1)} %convolution_divide_fusion.15), channel_id=1, source_target_pairs={{16,0},{32,16},{48,32},{64,48},{80,64},{96,80},{112,96},{128,112},... | collective-permute-start | bytes 12296 | tf_op jit(solution)/shard_map/ppermute | solution.py:29
  947.0 6.8 gather_fusion.6
  954.8 57.6 %all-reduce.2 = (f32[128,64]{1,0:T(8,128)S(1)}, f32[1]{0:T(128)}) all-reduce(f32[128,64]{1,0:T(8,128)S(1)} %fusion.73, f32[1]{0:T(128)} %bitcast.27), channel_id=1, replica_groups=mesh['leaf'=32,'vec'=16] {'vec'}, use_global_device_ids=true, to_apply=%region_17.19 | all-reduce | flops 8193 | bytes 65544 | tf_op jit(solution)/shard_map/psum | solution.py:107
  1018.3 6.8 gather_fusion.7
  1026.2 59.6 %all-reduce.1 = (f32[128,64]{1,0:T(8,128)S(1)}, f32[1]{0:T(128)}) all-reduce(f32[128,64]{1,0:T(8,128)S(1)} %fusion.71, f32[1]{0:T(128)} %bitcast.38), channel_id=1, replica_groups=mesh['leaf'=32,'vec'=16] {'vec'}, use_global_device_ids=true, to_apply=%region_20.22 | all-reduce | flops 8193 | bytes 65544 | tf_op jit(solution)/shard_map/psum | solution.py:107
  1093.2 6.8 gather_fusion.8
  1101.1 57.7 %all-reduce = (f32[128,64]{1,0:T(8,128)S(1)}, f32[1]{0:T(128)}) all-reduce(f32[128,64]{1,0:T(8,128)S(1)} %fusion.69, f32[1]{0:T(128)} %bitcast.49), channel_id=1, replica_groups=mesh['leaf'=32,'vec'=16] {'vec'}, use_global_device_ids=true, to_apply=%region_23.25 | all-reduce | flops 8193 | bytes 65544 | tf_op jit(solution)/shard_map/psum | solution.py:107
  1160.1 5.6 collective-permute-start.5
  1174.0 46.4 %collective-permute-start.7 = (f32[400,64]{0,1:T(8,128)S(1)}, f32[400,64]{0,1:T(8,128)S(1)}, u32[]{:S(2)}, u32[]{:S(2)}) collective-permute-start(f32[400,64]{0,1:T(8,128)S(1)} %broadcast_select_fusion.2), channel_id=1, source_target_pairs={{0,16},{16,32},{32,48},{48,64},{64,80},{80,96},{96,112},{112,128},... | collective-permute-start | bytes 307208 | tf_op jit(solution)/shard_map/ppermute | solution.py:29
  (300 shorter events, 147.0 us)
Async XLA Ops:
  7.2 1005.9 %copy-start = (f32[28,64,64]{2,1,0:T(8,128)S(1)}, f32[28,64,64]{2,1,0:T(8,128)}, u32[]{:S(2)}) copy-start(f32[28,64,64]{2,1,0:T(8,128)} %param.21) | copy-start | bytes 1376260
  7.2 22.0 %copy-start.3 = (bf16[16,16,256]{2,1,0:T(8,128)(2,1)S(1)}, bf16[16,16,256]{2,1,0:T(8,128)(2,1)}, u32[]{:S(2)}) copy-start(bf16[16,16,256]{2,1,0:T(8,128)(2,1)} %param.14) | copy-start | bytes 393220
  7.2 383.3 %all-reduce.9.cloned.1.call-start = ((), (), s32[]{:S(2)}) async-start(), calls=%async_computation | async-start | bytes 2097152 | tf_op jit(solution)/shard_map/psum | solution.py:107
  8.1 21.2 %copy-start.2 = (bf16[16,3,256]{2,0,1:T(8,128)(2,1)S(1)}, bf16[16,3,256]{2,0,1:T(8,128)(2,1)}, u32[]{:S(2)}) copy-start(bf16[16,3,256]{2,0,1:T(8,128)(2,1)} %param.13) | copy-start | bytes 73732
  9.1 20.1 %collective-permute-start = (bf16[16,19,256]{2,1,0:T(8,128)(2,1)S(1)}, bf16[16,19,256]{2,1,0:T(8,128)(2,1)S(1)}, u32[]{:S(2)}, u32[]{:S(2)}) collective-permute-start(bf16[16,19,256]{2,1,0:T(8,128)(2,1)S(1)} %pad_maximum_fusion.2), channel_id=1, source_target_pairs={{0,16},{16,32},{32,48},{48,64},{64,80},{80,96},{96,112},{112,128},... | collective-permute-start | bytes 466952 | tf_op jit(solution)/shard_map/ppermute | solution.py:20
  14.0 15.2 %collective-permute-start.1 = (bf16[16,19,256]{2,1,0:T(8,128)(2,1)S(1)}, bf16[16,19,256]{2,1,0:T(8,128)(2,1)S(1)}, u32[]{:S(2)}, u32[]{:S(2)}) collective-permute-start(bf16[16,19,256]{2,1,0:T(8,128)(2,1)S(1)} %pad_maximum_fusion.2), channel_id=1, source_target_pairs={{16,0},{32,16},{48,32},{64,48},{80,64},{96,80},{112,96},{128,112},... | collective-permute-start | bytes 466952 | tf_op jit(solution)/shard_map/ppermute | solution.py:21
  108.8 161.1 %copy-start.4 = (s32[16,64]{1,0:T(8,128)S(1)}, s32[16,64]{1,0:T(8,128)}, u32[]{:S(2)}) copy-start(s32[16,64]{1,0:T(8,128)} %param.16) | copy-start | bytes 12292
  271.9 118.5 %copy-start.6 = (f32[16,64,64]{2,1,0:T(8,128)S(1)}, f32[16,64,64]{2,1,0:T(8,128)}, u32[]{:S(2)}) copy-start(f32[16,64,64]{2,1,0:T(8,128)} %param.17) | copy-start | bytes 786436
  272.0 304.0 %all-reduce.11.cloned.1.call-start = ((), (), s32[]{:S(2)}) async-start(), calls=%async_computation.1 | async-start | bytes 524288 | tf_op jit(solution)/shard_map/psum | solution.py:107
  392.8 67.0 %copy-start.1 = (f32[16,256,64]{1,2,0:T(8,128)}, f32[16,256,64]{1,2,0:T(8,128)S(1)}, u32[]{:S(2)}) copy-start(f32[16,256,64]{1,2,0:T(8,128)S(1)} %convolution_divide_fusion) | copy-start | bytes 3145732
  394.0 182.0 %copy-start.5 = (f32[15,64,64]{2,1,0:T(8,128)S(1)}, f32[15,64,64]{2,1,0:T(8,128)}, u32[]{:S(2)}) copy-start(f32[15,64,64]{2,1,0:T(8,128)} %param.19) | copy-start | bytes 737284
  461.3 263.7 %all-reduce.13.cloned.1.call-start = ((), (), s32[]{:S(2)}) async-start(), calls=%async_computation.2 | async-start | bytes 262144 | tf_op jit(solution)/shard_map/psum | solution.py:107
  612.6 243.4 %all-reduce.15.cloned.1.call-start = ((), (), s32[]{:S(2)}) async-start(), calls=%async_computation.3 | async-start | bytes 131072 | tf_op jit(solution)/shard_map/psum | solution.py:107
  926.3 20.6 %collective-permute-start.2 = (f32[16,64]{1,0:T(8,128)S(1)}, f32[16,64]{1,0:T(8,128)S(1)}, u32[]{:S(2)}, u32[]{:S(2)}) collective-permute-start(f32[16,64]{1,0:T(8,128)S(1)} %convolution_divide_fusion.15), channel_id=1, source_target_pairs={{16,0},{32,16},{48,32},{64,48},{80,64},{96,80},{112,96},{128,112},... | collective-permute-start | bytes 12296 | tf_op jit(solution)/shard_map/ppermute | solution.py:29
  1013.5 4.7 collective-permute-start.3
  1086.8 6.3 collective-permute-start.4
  1160.1 7.5 collective-permute-start.5
  1167.6 6.4 collective-permute-start.6
  1174.0 48.4 %collective-permute-start.7 = (f32[400,64]{0,1:T(8,128)S(1)}, f32[400,64]{0,1:T(8,128)S(1)}, u32[]{:S(2)}, u32[]{:S(2)}) collective-permute-start(f32[400,64]{0,1:T(8,128)S(1)} %broadcast_select_fusion.2), channel_id=1, source_target_pairs={{0,16},{16,32},{32,48},{48,64},{64,80},{80,96},{96,112},{112,128},... | collective-permute-start | bytes 307208 | tf_op jit(solution)/shard_map/ppermute | solution.py:29
Sparse Core Ops, SparseCore 0:
  272.1 118.3 all-reduce.8
  461.4 114.5 all-reduce.10
  612.7 112.1 all-reduce.12
  744.8 111.1 all-reduce.14
where the time goes:
time: 1230 us
  blocking collectives  359 us (29%)
  waiting for transfers between devices  347 us (28%)
  local copies, waits for them, and re-layouts  319 us (26%)
  starting transfers between devices  87.7 us (7%)
  matrix products  83.5 us (7%)
  between operations  17.1 us (1%)
  other arithmetic  15.4 us (1%)
    psum x8, blocking collectives, combine_stats(): return lax.psum((gram_rows, squares), 'vec')  359 us
    psum x4, waiting for transfers between devices, combine_stats(): return lax.psum((gram_rows, squares), 'vec')  332 us
    gather x24, local copies, waits for them, and re-layouts, interpolate(): chosen = jnp.take_along_axis(sketch, index_grid, axis=2)  305 us
    ppermute x6, starting transfers between devices, shifted(): return lax.ppermute(shard, axis, pairs)  77.4 us
    dot_general x16, matrix products, add_slot(): jnp.einsum('nsq,npq->nsp', blocks[:, 3:], kernel_block, preferred_element...  66.5 us
  transfers between devices with their start and end apart: 12, of which 10 were waited for; matrix products, arithmetic and copies ran while one was open for 1% of the time, Pallas kernels for 0%

commit v1 on v0

v1 whole, which is shorter than its diff:
```python
import functools

import jax
import jax.numpy as jnp
from jax import lax
from jax.experimental import pallas as pl
from jax.experimental.pallas import tpu as pltpu
from jax.sharding import PartitionSpec as P

UPL = 3
SOFTEN = 0.0009
EPSILON = 1e-06
F32 = jnp.float32
BF16 = jnp.bfloat16
NN = (((1,), (0,)), ((), ()))
NT = (((1,), (1,)), ((), ()))


def mm(a, b, dims=NN):
    return lax.dot_general(a, b, dims, preferred_element_type=F32)


def split(a):
    high = a.astype(BF16)
    return high, (a - high.astype(F32)).astype(BF16)


def mm3(a, b, dims=NN):
    return mm(a[0], b[0], dims) + (mm(a[0], b[1], dims) + mm(a[1], b[0], dims))


def feature_rows(xyz, weight):
    norm = SOFTEN / 2 + xyz[0] * xyz[0] + xyz[1] * xyz[1] + xyz[2] * xyz[2]
    high = norm.astype(BF16).astype(F32)
    rest = norm - high
    middle = rest.astype(BF16).astype(F32)
    low = (rest - middle).astype(BF16).astype(F32)
    return [part * weight for part in (high, middle, low)]


def body(
    leaf_n,
    vec_n,
    axes,
    pts,
    probe,
    nbr,
    leaf_piv,
    leaf_inv,
    local_piv,
    local_inv,
    upper_piv,
    upper_inv,
    out_leaf,
    out_local,
    out_upper,
    out_top,
    ext_pts,
    ext_probe,
    near,
    far,
    inv,
    weights,
    sketches,
    z_ref,
    joined,
    z_top,
    leaf_map,
    node_maps,
    inv_sem,
    own_sem,
    side_send,
    side_recv,
    sk_send,
    sk_recv,
    up_send,
    up_recv,
    map_send,
    map_recv,
    out_sem,
):
    leaf_axis, vec_axis = axes
    d = lax.axis_index(leaf_axis)
    v = lax.axis_index(vec_axis)
    levels = vec_n.bit_length() - 1
    columns = probe.shape[1]
    points = probe.shape[2]
    total = columns * vec_n

    def on_vec(u):
        return {leaf_axis: d, vec_axis: u}

    def on_leaf(g):
        return {leaf_axis: g, vec_axis: v}

    def remote(src, dst, send, recv, target):
        return pltpu.make_async_remote_copy(
            src_ref=src,
            dst_ref=dst,
            send_sem=send,
            recv_sem=recv,
            device_id=target,
            device_id_type=pl.DeviceIdType.MESH,
        )

    def flip(index, stride):
        return index + stride * (1 - 2 * ((index // stride) % 2))

    before = (d + leaf_n - 1) % leaf_n
    after = (d + 1) % leaf_n
    upper_partner = [flip(d, 1 << u) for u in range(UPL)]

    barrier = pltpu.get_barrier_semaphore()
    targets = [on_vec((v + t) % vec_n) for t in range(1, vec_n)]
    targets += [on_leaf(g) for g in [before, after] + upper_partner[1:]]
    for target in targets:
        pl.semaphore_signal(
            barrier, inc=1, device_id=target, device_id_type=pl.DeviceIdType.MESH
        )

    rows = [(leaf_piv, leaf_inv, v)]
    offset = 0
    for t in range(1, levels + 1):
        rows.append((local_piv, local_inv, offset + v // (1 << t)))
        offset += vec_n >> t
    offset = 0
    for u in range(1, UPL + 1):
        rows.append((upper_piv, upper_inv, offset + d // (1 << u)))
        offset += leaf_n >> u
    inv_copies = [
        pltpu.make_async_copy(source.at[row], inv.at[n], inv_sem.at[n])
        for n, (_, source, row) in enumerate(rows)
    ]
    for copy in inv_copies:
        copy.start()
    own_pts = pltpu.make_async_copy(pts, ext_pts.at[1], own_sem.at[0])
    own_probe = pltpu.make_async_copy(
        probe, ext_probe.at[pl.ds(vec_n, vec_n)], own_sem.at[1]
    )
    own_pts.start()
    own_probe.start()

    pl.semaphore_wait(barrier, len(targets))

    sides = []
    for n, (target, place) in enumerate([(after, 0), (before, 2)]):
        sides.append(
            remote(
                pts,
                ext_pts.at[place],
                side_send.at[2 * n],
                side_recv.at[2 * n],
                on_leaf(target),
            )
        )
        sides.append(
            remote(
                probe,
                ext_probe.at[pl.ds(place * vec_n, vec_n)],
                side_send.at[2 * n + 1],
                side_recv.at[2 * n + 1],
                on_leaf(target),
            )
        )
    for copy in sides:
        copy.start()

    for n, (pivots, _, row) in enumerate(rows):
        inv_copies[n].wait()
        size = points if n == 0 else 2 * inv.shape[1]
        chosen = pivots[pl.ds(row, 1), :]
        spread = (
            lax.broadcasted_iota(jnp.int32, (size, chosen.shape[1]), 0) == chosen
        ).astype(F32).astype(BF16)
        high, low = split(jnp.transpose(inv[n]))
        weights[n, 0, :, :size] = mm(high, spread, NT).astype(BF16)
        weights[n, 1, :, :size] = mm(low, spread, NT).astype(BF16)

    own_pts.wait()
    own_probe.wait()

    def features(side):
        xyz = [ext_pts[side, c].astype(F32) for c in range(3)]
        norm = feature_rows(xyz, 4096.0)
        one = jnp.ones((1, points), F32)
        pad = jnp.zeros((7, points), F32)
        for r in range(vec_n):
            at = [x[r : r + 1] for x in xyz]
            nm = [x[r : r + 1] for x in norm]
            if side == 1:
                near[r] = jnp.concatenate(at + nm + [one] * 3 + [pad], axis=0).astype(BF16)
            rows_far = [x * -8192.0 for x in at] + [one] * 3 + nm + [pad]
            far[side * vec_n + r] = jnp.transpose(
                jnp.concatenate(rows_far, axis=0)
            ).astype(BF16)

    features(1)
    for copy in sides[0:2]:
        copy.wait_recv()
    features(0)
    for copy in sides[2:4]:
        copy.wait_recv()
    features(2)

    first = (d - 1) * vec_n

    def sketch_of(c):
        near_c = near[c]

        def slot(k, acc):
            listed = nbr[c, k]
            place = jnp.clip(listed - first, 0, 3 * vec_n - 1)
            distance = mm(far[place], near_c)
            tile = lax.rsqrt(distance).astype(BF16)
            vectors = ext_probe[place]
            vectors = jnp.where(listed >= 0, vectors, jnp.zeros_like(vectors))
            return acc + mm(vectors, tile)

        return lax.fori_loop(
            0, nbr.shape[1], slot, jnp.zeros((columns, points), F32), unroll=4
        )

    def sketch_copy(t):
        return remote(
            sketches.at[t],
            z_ref.at[pl.ds(pl.multiple_of(v * columns, columns), columns)],
            sk_send.at[t],
            sk_recv.at[t],
            on_vec((v + 1 + t) % vec_n),
        )

    @pl.loop(0, vec_n - 1)
    def _(t):
        sketches[t] = sketch_of((v + 1 + t) % vec_n)
        sketch_copy(t).start()

    z_ref[pl.ds(pl.multiple_of(v * columns, columns), columns), :] = sketch_of(v)

    @pl.loop(0, vec_n - 1)
    def _(t):
        sketch_copy(t).wait()

    def node(n, z, zt):
        size = zt.shape[0]
        z_parts, zt_parts = split(z), split(zt)
        mean_sq = jnp.sum(z * z) / (size * total) + EPSILON
        gram = split(mm3(zt_parts, z_parts))
        w = (weights[n, 0, :, :size], weights[n, 1, :, :size])
        interp = mm3(w, gram) / (total * mean_sq)
        return interp, mean_sq, zt_parts

    def up_of(interp, mean_sq, zt_parts):
        return mm3(split(interp), zt_parts) * lax.rsqrt(mean_sq)

    map_copies = []
    count = 0

    def send_map(source, out, place, level, count):
        step = 1 << level
        for j in range(1, vec_n >> level):
            map_copies.append(
                remote(
                    source,
                    out.at[place],
                    map_send.at[count],
                    map_recv.at[count],
                    on_vec((v + j * step) % vec_n),
                )
            )
            map_copies[-1].start()
            count += 1
        return count

    own_copies = []

    def own_map(source, target, sem):
        own_copies.append(pltpu.make_async_copy(source, target, sem))
        own_copies[-1].start()

    z = z_ref[...]
    interp, mean_sq, zt_parts = node(0, z, jnp.transpose(z))
    leaf_map[...] = interp
    up = up_of(interp, mean_sq, zt_parts)

    offset = 0
    pending = (leaf_map, out_leaf, v, 0)
    for n in range(1, levels + UPL + 1):
        if n <= levels:
            stride = 1 << (n - 1)
            half = (v // stride) % 2
            if n % 2 == 1:
                partner = on_vec(flip(v, stride))
            else:
                partner = on_vec(flip(flip(v, stride), stride // 2))
        else:
            stride = 1 << (n - levels - 1)
            half = (d // stride) % 2
            partner = on_leaf(upper_partner[n - levels - 1])
        joined[n - 1, half] = up
        exchange = remote(
            joined.at[n - 1, half],
            joined.at[n - 1, half],
            up_send.at[n - 1],
            up_recv.at[n - 1],
            partner,
        )
        exchange.start()
        if pending is not None:
            source, out, place, level = pending
            own_map(source, out.at[place], out_sem.at[n - 1])
            count = send_map(source, out, place, level, count)
        exchange.wait()
        zt = joined[n - 1].reshape(2 * joined.shape[2], total)
        z = jnp.transpose(zt)
        interp, mean_sq, zt_parts = node(n, z, zt)
        node_maps[n - 1] = interp
        if n <= levels:
            pending = (node_maps.at[n - 1], out_local, offset + v // (1 << n), n)
            offset += vec_n >> n
        else:
            pending = None
            own_map(
                node_maps.at[n - 1], out_upper.at[0, n - levels - 1], out_sem.at[n]
            )
        if n < levels + UPL:
            up = up_of(interp, mean_sq, zt_parts)
        else:
            z_top[...] = z
            mine = z_top[pl.ds(pl.multiple_of(v * columns, columns), columns), :]
            out_top[0] = mm3(split(mine), split(interp), NT) * lax.rsqrt(mean_sq)

    for copy in sides:
        copy.wait_send()
    for copy in own_copies:
        copy.wait()
    for copy in map_copies:
        copy.wait()


def on_device(
    leaf_n,
    vec_n,
    axes,
    points,
    probe_vectors,
    neighbours,
    leaf_pivots,
    leaf_inverse,
    local_pivots,
    local_inverse,
    upper_pivots,
    upper_inverse,
):
    group, columns, size = probe_vectors.shape
    rank = leaf_pivots.shape[1]
    slots = neighbours.shape[1]
    levels = vec_n.bit_length() - 1
    total = columns * vec_n
    nodes = levels + UPL
    maps = sum((vec_n >> t) - 1 for t in range(levels))
    vmem = pl.BlockSpec(memory_space=pltpu.VMEM)
    anywhere = pl.BlockSpec(memory_space=pl.ANY)
    smem = pl.BlockSpec(memory_space=pltpu.SMEM)
    dma = pltpu.SemaphoreType.DMA
    leaf_map, local_map, upper_map, top = pl.pallas_call(
        functools.partial(body, leaf_n, vec_n, axes),
        out_shape=(
            jax.ShapeDtypeStruct((group, rank, size), F32),
            jax.ShapeDtypeStruct((group - 1, rank, 2 * rank), F32),
            jax.ShapeDtypeStruct((1, UPL, rank, 2 * rank), F32),
            jax.ShapeDtypeStruct((1, columns, rank), F32),
        ),
        in_specs=[anywhere, anywhere, smem, vmem, anywhere, vmem, anywhere, vmem, anywhere],
        out_specs=(anywhere, anywhere, anywhere, vmem),
        scratch_shapes=[
            pltpu.VMEM((3, 3, group, size), BF16),
            pltpu.VMEM((3 * group, columns, size), BF16),
            pltpu.VMEM((group, 16, size), BF16),
            pltpu.VMEM((3 * group, size, 16), BF16),
            pltpu.VMEM((nodes + 1, rank, rank), F32),
            pltpu.VMEM((nodes + 1, 2, rank, size), BF16),
            pltpu.VMEM((vec_n - 1, columns, size), F32),
            pltpu.VMEM((total, size), F32),
            pltpu.VMEM((nodes, 2, rank, total), F32),
            pltpu.VMEM((total, 2 * rank), F32),
            pltpu.VMEM((rank, size), F32),
            pltpu.VMEM((nodes, rank, 2 * rank), F32),
            dma((nodes + 1,)),
            dma((2,)),
            dma((4,)),
            dma((4,)),
            dma((vec_n - 1,)),
            dma((vec_n - 1,)),
            dma((nodes,)),
            dma((nodes,)),
            dma((maps,)),
            dma((maps,)),
            dma((nodes + 1,)),
        ],
        compiler_params=pltpu.CompilerParams(
            collective_id=0, has_side_effects=True, vmem_limit_bytes=48 * 2**20
        ),
    )(
        jnp.transpose(points, (1, 0, 2)),
        probe_vectors,
        neighbours,
        leaf_pivots,
        leaf_inverse,
        local_pivots,
        local_inverse,
        upper_pivots,
        upper_inverse,
    )
    return (
        jnp.swapaxes(leaf_map, 1, 2),
        jnp.swapaxes(local_map, 1, 2),
        jnp.swapaxes(upper_map, 2, 3),
        top,
    )


def solution(mesh):
    axes = tuple(mesh.axis_names)
    placed = (
        P("leaf", None, None),
        P("leaf", "vec", None),
        P("leaf", None),
        P("leaf", None),
        P("leaf", None, None),
        P("leaf", None),
        P("leaf", None, None),
        P(),
        P(),
    )
    return jax.shard_map(
        functools.partial(on_device, mesh.shape["leaf"], mesh.shape["vec"], axes),
        mesh=mesh,
        in_specs=placed,
        out_specs=(
            P("leaf", None, None),
            P("leaf", None, None),
            P("leaf", None, None, None),
            P("leaf", "vec", None),
        ),
        check_vma=False,
    )
```

time: 1230 us -> 104 us (0.08)
  blocking collectives: 359 us -> 0 us
  waiting for transfers between devices: 347 us -> 0 us
  local copies, waits for them, and re-layouts: 319 us -> 10.7 us
  Pallas kernels: 0 us -> 92.5 us
  starting transfers between devices: 87.7 us -> 0 us
  matrix products: 83.5 us -> 0 us
  between operations: 17.1 us -> 0.66 us
  other arithmetic: 15.4 us -> 0 us
    psum x8 -> x0, blocking collectives: 359 us -> none  [combine_stats(): return lax.psum((gram_rows, squares), 'vec')]
    psum x4 -> x0, waiting for transfers between devices: 332 us -> none  [combine_stats(): return lax.psum((gram_rows, squares), 'vec')]
    gather x40 -> x0, local copies, waits for them, and re-layouts: 314 us -> none  [the longest x24 305 us: interpolate(): chosen = jnp.take_along_axis(sketch, index_grid, axis=2)]
    pallas_call x0 -> x1, Pallas kernels: none -> 92.5 us  [on_device(): pl.pallas_call(functools.partial(body, leaf_n, vec_n, axes), out_shape=(j...]
    ppermute x8 -> x0, starting transfers between devices: 87.5 us -> none  [the longest x6 77.4 us: shifted(): return lax.ppermute(shard, axis, pairs)]
    dot_general x40 -> x0, matrix products: 83.5 us -> none  [the longest x16 66.5 us: add_slot(): jnp.einsum('nsq,npq->nsp', blocks[:, 3:], kernel_block, preferred_element...]
    ppermute x8 -> x0, waiting for transfers between devices: 15.4 us -> none  [the longest x6 15.4 us: shifted(): return lax.ppermute(shard, axis, pairs)]
  transfers between devices with their start and end apart: 12 -> 0, of which waited for: 10 -> 0; matrix products, arithmetic and copies ran while one was open for 1% -> 0% of each run, Pallas kernels for 0% -> 0%
where the time goes in v1:
time: 104 us
  Pallas kernels  92.5 us (89%)
  local copies, waits for them, and re-layouts  10.7 us (10%)
    pallas_call x1, Pallas kernels, on_device(): pl.pallas_call(functools.partial(body, leaf_n, vec_n, axes), out_shape=(j...  92.5 us
    unnamed x22, local copies, waits for them, and re-layouts  10.7 us

profile of v1, /device:TPU:1, one launch (start us, length us, event | category | flops | bytes accessed | tf_op | source)
XLA Modules:
  0.0 103.9 jit_solution(10254481721703116278)
XLA Ops:
  0.6 0.0 copy-start
  0.6 1.2 %copy-done = f32[28,64,64]{2,1,0:T(8,128)S(1)} copy-done((f32[28,64,64]{2,1,0:T(8,128)S(1)}, f32[28,64,64]{2,1,0:T(8,128)}, u32[]{:S(2)}) %copy-start) | copy-done | bytes 458776
  1.8 0.0 copy-start.1
  1.8 1.0 %copy-done.1 = f32[16,64,64]{2,1,0:T(8,128)S(1)} copy-done((f32[16,64,64]{2,1,0:T(8,128)S(1)}, f32[16,64,64]{2,1,0:T(8,128)}, u32[]{:S(2)}) %copy-start.1) | copy-done | bytes 262168
  2.9 0.0 copy-start.2
  2.9 1.0 copy-done.2
  3.9 0.0 copy-start.3
  3.9 0.9 copy-done.3
  4.8 0.0 copy-start.4
  4.8 0.7 copy-done.4
  5.5 0.0 copy-start.5
  5.5 0.7 copy-done.5
  6.2 0.0 copy-start.6
  6.2 0.7 copy-done.6
  6.9 0.0 copy-start.7
  6.9 0.7 copy-done.7
  7.6 0.0 copy-start.8
  7.6 0.7 copy-done.8
  8.3 92.5 %shard_map.120 = (f32[16,64,256]{2,1,0:T(8,128)S(1)}, f32[15,64,128]{2,1,0:T(8,128)S(1)}, f32[1,3,64,128]{3,2,1,0:T(8,128)S(1)}, f32[1,16,64]{2,1,0:T(8,128)S(1)}) custom-call(bf16[3,16,256]{2,1,0:T(8,128)(2,1)S(1)} %bitcast.7, bf16[16,16,256]{2,1,0:T(8,128)(2,1)S(1)} %copy-done.3, s32[16,16]{1,0:T(8,128)S(1)} %copy-done.6, s32[16,64]{1,0:T(8,128)S(1)} %copy-done.7, ...), custom_call_target="tpu_custom_call" | custom-call | tf_op jit(solution)/shard_map/pallas_call | solution.py:365
  100.9 1.0 copy.17
  101.8 0.8 copy.18
  102.6 0.6 copy.19
  103.3 0.6 copy.20
Async XLA Ops:
  0.6 1.2 %copy-start = (f32[28,64,64]{2,1,0:T(8,128)S(1)}, f32[28,64,64]{2,1,0:T(8,128)}, u32[]{:S(2)}) copy-start(f32[28,64,64]{2,1,0:T(8,128)} %upper_inv.1) | copy-start | bytes 1376260
  1.8 1.0 %copy-start.1 = (f32[16,64,64]{2,1,0:T(8,128)S(1)}, f32[16,64,64]{2,1,0:T(8,128)}, u32[]{:S(2)}) copy-start(f32[16,64,64]{2,1,0:T(8,128)} %leaf_inv.1) | copy-start | bytes 786436
  2.9 1.0 copy-start.2
  3.9 0.9 copy-start.3
  4.8 0.7 copy-start.4
  5.5 0.7 copy-start.5
  6.2 0.7 copy-start.6
  6.9 0.7 copy-start.7
  7.6 0.7 copy-start.8

commit v2 on v1

v2 whole, which is shorter than its diff:
```python
import functools

import jax
import jax.numpy as jnp
from jax import lax
from jax.experimental import pallas as pl
from jax.experimental.pallas import tpu as pltpu
from jax.sharding import PartitionSpec as P

UPL = 3
SOFTEN = 0.0009
EPSILON = 1e-06
FLUSH = 4
F32 = jnp.float32
BF16 = jnp.bfloat16
NN = (((1,), (0,)), ((), ()))
NT = (((1,), (1,)), ((), ()))


def mm(a, b, dims=NN):
    return lax.dot_general(a, b, dims, preferred_element_type=F32)


def split(a):
    high = a.astype(BF16)
    return high, (a - high.astype(F32)).astype(BF16)


def mm3(a, b, dims=NN):
    return mm(a[0], b[0], dims) + (mm(a[0], b[1], dims) + mm(a[1], b[0], dims))


def feature_rows(xyz, weight):
    norm = SOFTEN / 2 + xyz[0] * xyz[0] + xyz[1] * xyz[1] + xyz[2] * xyz[2]
    high = norm.astype(BF16).astype(F32)
    rest = norm - high
    middle = rest.astype(BF16).astype(F32)
    low = (rest - middle).astype(BF16).astype(F32)
    return [part * weight for part in (high, middle, low)]


def body(
    leaf_n,
    vec_n,
    axes,
    pts,
    probe,
    nbr_in,
    leaf_piv,
    leaf_inv,
    local_piv,
    local_inv,
    upper_piv,
    upper_inv,
    out_leaf,
    out_local,
    out_upper,
    out_top,
    nbr,
    piv,
    ext_pts,
    ext_probe,
    near,
    far,
    tiles,
    vectors,
    inv,
    weights,
    sketches,
    z_ref,
    joined,
    z_top,
    leaf_map,
    node_maps,
    top_ref,
    inv_sem,
    piv_sem,
    own_sem,
    side_send,
    side_recv,
    sk_send,
    sk_recv,
    up_send,
    up_recv,
    map_send,
    map_recv,
    out_sem,
):
    leaf_axis, vec_axis = axes
    d = lax.axis_index(leaf_axis)
    v = lax.axis_index(vec_axis)
    group, columns, points = probe.shape
    rank = inv.shape[1]
    levels = group.bit_length() - 1
    total = columns * vec_n
    wide = 2 * columns
    slots = nbr.shape[1]
    part = group // 2

    x, y = v % 4, v // 4
    pair, side_row = x // 2, x % 2
    half = ((x + 1) // 2) % 2
    w = part * half + 4 * pair + y

    def vec_of(cluster):
        high, low = cluster // part, (cluster // 4) % 2
        return 4 * (cluster % 4) + 2 * low + (high + low) % 2

    def on_vec(u):
        return {leaf_axis: d, vec_axis: u}

    def on_leaf(g):
        return {leaf_axis: g, vec_axis: v}

    def remote(src, dst, send, recv, target):
        return pltpu.make_async_remote_copy(
            src_ref=src,
            dst_ref=dst,
            send_sem=send,
            recv_sem=recv,
            device_id=target,
            device_id_type=pl.DeviceIdType.MESH,
        )

    def flip(index, stride):
        return index + stride * (1 - 2 * ((index // stride) % 2))

    before = (d + leaf_n - 1) % leaf_n
    after = (d + 1) % leaf_n
    upper_partner = [flip(d, 1 << u) for u in range(UPL)]

    barrier = pltpu.get_barrier_semaphore()
    targets = [on_vec((v + t) % vec_n) for t in range(1, vec_n)]
    targets += [on_leaf(g) for g in [before, after] + upper_partner[1:]]
    for target in targets:
        pl.semaphore_signal(
            barrier, inc=1, device_id=target, device_id_type=pl.DeviceIdType.MESH
        )

    mine = [
        pltpu.make_async_copy(pts, ext_pts.at[1], own_sem.at[0]),
        pltpu.make_async_copy(nbr_in, nbr, own_sem.at[1]),
        pltpu.make_async_copy(
            probe,
            ext_probe.at[
                pl.ds(group, group),
                pl.ds(pl.multiple_of(columns * side_row, columns), columns),
            ],
            own_sem.at[2],
        ),
    ]
    for copy in mine:
        copy.start()
    rows = [(0, leaf_inv, v * 0 + w, w)]
    offset = 0
    for t in range(1, levels + 1):
        place = offset + w // (1 << t)
        rows.append((1, local_inv, place, place))
        offset += group >> t
    offset = 0
    for u in range(1, UPL + 1):
        place = offset + d // (1 << u)
        rows.append((2, upper_inv, place, place))
        offset += leaf_n >> u
    inv_copies = [
        pltpu.make_async_copy(source.at[row], inv.at[n], inv_sem.at[n])
        for n, (_, source, row, _) in enumerate(rows)
    ]
    piv_copies = [
        pltpu.make_async_copy(
            source, piv.at[n, pl.ds(0, source.shape[0])], piv_sem.at[n]
        )
        for n, source in enumerate((leaf_piv, local_piv, upper_piv))
    ]
    for copy in piv_copies + inv_copies:
        copy.start()

    pl.semaphore_wait(barrier, len(targets))

    def strip(place, row):
        return ext_probe.at[
            pl.ds(place * group, group),
            pl.ds(pl.multiple_of(columns * row, columns), columns),
        ]

    ways = [(after, 0), (before, 2)]
    pts_copies = [
        remote(pts, ext_pts.at[place], side_send.at[n], side_recv.at[n], on_leaf(target))
        for n, (target, place) in enumerate(ways)
    ]
    pair_copy = remote(
        probe, strip(1, side_row), side_send.at[2], side_recv.at[2], on_vec(flip(v, 1))
    )
    direct = [
        remote(
            probe,
            strip(place, side_row),
            side_send.at[3 + n],
            side_recv.at[3 + n],
            on_leaf(target),
        )
        for n, (target, place) in enumerate(ways)
    ]
    passed = [
        remote(
            strip(1, 1 - side_row),
            strip(place, 1 - side_row),
            side_send.at[5 + n],
            side_recv.at[5 + n],
            on_leaf(target),
        )
        for n, (target, place) in enumerate(ways)
    ]
    for copy in pts_copies + [pair_copy] + direct:
        copy.start()

    def features(side):
        xyz = [ext_pts[side, c].astype(F32) for c in range(3)]
        norm = feature_rows(xyz, 4096.0)
        one = jnp.ones((1, points), F32)
        pad = jnp.zeros((7, points), F32)
        for r in range(group):
            at = [q[r : r + 1] for q in xyz]
            nm = [q[r : r + 1] for q in norm]
            if side == 1:
                near[r] = jnp.concatenate(at + nm + [one] * 3 + [pad], axis=0).astype(BF16)
            rows_far = [q * -8192.0 for q in at] + [one] * 3 + nm + [pad]
            far[side * group + r] = jnp.transpose(
                jnp.concatenate(rows_far, axis=0)
            ).astype(BF16)

    mine[0].wait()
    features(1)
    pts_copies[0].wait_recv()
    features(0)
    pts_copies[1].wait_recv()
    features(2)
    mine[1].wait()

    first = (d - 1) * group

    def place_of(c, k):
        listed = nbr[c, k]
        return jnp.clip(listed - first, 0, 3 * group - 1), listed >= 0

    def tiles_of(c):
        cluster = half * part + c
        near_c = near[cluster]
        for k in range(slots):
            place, _ = place_of(cluster, k)
            tiles[c, k * points : (k + 1) * points, :] = lax.rsqrt(
                mm(far[place], near_c)
            ).astype(BF16)

    pl.loop(0, 2)(tiles_of)
    mine[2].wait()
    pair_copy.wait_recv()
    for copy in passed:
        copy.start()
    pl.loop(2, part)(tiles_of)

    for copy in piv_copies:
        copy.wait()
    for n, (which, _, _, row) in enumerate(rows):
        inv_copies[n].wait()
        size = points if n == 0 else 2 * rank
        chosen = piv[which, pl.ds(row, 1), :]
        spread = (
            lax.broadcasted_iota(jnp.int32, (size, rank), 0) == chosen
        ).astype(F32).astype(BF16)
        high, low = split(jnp.transpose(inv[n]))
        weights[n, 0, :, :size] = mm(high, spread, NT).astype(BF16)
        weights[n, 1, :, :size] = mm(low, spread, NT).astype(BF16)

    for copy in direct + passed:
        copy.wait_recv()

    z_rows = pl.ds(pl.multiple_of(wide * (2 * y + pair), wide), wide)
    own = w % part

    def sketch_of(c):
        for k in range(slots):
            place, listed = place_of(half * part + c, k)
            block = ext_probe[place]
            vectors[:, k * points : (k + 1) * points] = jnp.where(
                listed, block, jnp.zeros_like(block)
            )
        return mm(vectors[...], tiles[c])

    def sketch_copy(t):
        c = (own + 1 + t) % part
        return c, remote(
            sketches.at[t],
            z_ref.at[z_rows],
            sk_send.at[t],
            sk_recv.at[t],
            on_vec(vec_of(half * part + c)),
        )

    @pl.loop(0, part - 1)
    def _(t):
        c, copy = sketch_copy(t)
        sketches[t] = sketch_of(c)
        copy.start()

    z_ref[z_rows, :] = sketch_of(own)

    @pl.loop(0, part - 1)
    def _(t):
        sketch_copy(t)[1].wait()

    def node(n, z, zt):
        size = zt.shape[0]
        z_parts, zt_parts = split(z), split(zt)
        mean_sq = jnp.sum(z * z) / (size * total) + EPSILON
        gram = split(mm3(zt_parts, z_parts))
        scattered = (weights[n, 0, :, :size], weights[n, 1, :, :size])
        interp = mm3(scattered, gram) / (total * mean_sq)
        return interp, mean_sq, zt_parts

    def up_of(interp, mean_sq, zt_parts):
        return mm3(split(interp), zt_parts) * lax.rsqrt(mean_sq)

    map_copies = []
    own_copies = []

    def send_map(source, out, place, level):
        own_copies.append(
            pltpu.make_async_copy(source, out.at[place], out_sem.at[len(own_copies)])
        )
        own_copies[-1].start()
        step = 1 << level
        for j in range(1, group >> level):
            n = len(map_copies)
            map_copies.append(
                remote(
                    source,
                    out.at[place],
                    map_send.at[n],
                    map_recv.at[n],
                    on_vec(vec_of((w + j * step) % group)),
                )
            )
            map_copies[-1].start()

    z = z_ref[...]
    interp, mean_sq, zt_parts = node(0, z, jnp.transpose(z))
    leaf_map[...] = interp
    up = up_of(interp, mean_sq, zt_parts)

    offset = 0
    pending = [(leaf_map, out_leaf, w, 0)]
    for n in range(1, levels + UPL + 1):
        if n <= levels:
            stride = 1 << (n - 1)
            branch = (w // stride) % 2
            other = flip(w, stride)
            if n == 2:
                other = flip(other, 1)
            partner = on_vec(vec_of(other))
        else:
            stride = 1 << (n - levels - 1)
            branch = (d // stride) % 2
            partner = on_leaf(upper_partner[n - levels - 1])
        joined[n - 1, branch] = up
        exchange = remote(
            joined.at[n - 1, branch],
            joined.at[n - 1, branch],
            up_send.at[n - 1],
            up_recv.at[n - 1],
            partner,
        )
        exchange.start()
        if n >= FLUSH:
            for item in pending:
                send_map(*item)
            pending = []
        exchange.wait()
        zt = joined[n - 1].reshape(2 * rank, total)
        z = jnp.transpose(zt)
        interp, mean_sq, zt_parts = node(n, z, zt)
        node_maps[n - 1] = interp
        if n <= levels:
            pending.append((node_maps.at[n - 1], out_local, offset + w // (1 << n), n))
            offset += group >> n
        else:
            own_copies.append(
                pltpu.make_async_copy(
                    node_maps.at[n - 1],
                    out_upper.at[0, n - levels - 1],
                    out_sem.at[len(own_copies)],
                )
            )
            own_copies[-1].start()
        if n < levels + UPL:
            up = up_of(interp, mean_sq, zt_parts)
        else:
            z_top[...] = z
            kept = z_top[pl.ds(pl.multiple_of(v * columns, columns), columns), :]
            top_ref[0] = mm3(split(kept), split(interp), NT) * lax.rsqrt(mean_sq)
            own_copies.append(
                pltpu.make_async_copy(top_ref, out_top, out_sem.at[len(own_copies)])
            )
            own_copies[-1].start()

    for copy in pts_copies + [pair_copy] + direct + passed:
        copy.wait_send()
    for copy in own_copies:
        copy.wait()
    for copy in map_copies:
        copy.wait()


def write_out(a, b, c, e, out_a, out_b, out_c, out_e, buf_a, buf_b, buf_c, buf_e, in_sem, out_sem):
    pieces = []
    for source, buf, target, step in (
        (a, buf_a, out_a, 4),
        (b, buf_b, out_b, 5),
        (c, buf_c, out_c, 1),
        (e, buf_e, out_e, 1),
    ):
        for start in range(0, source.shape[0], step):
            at = pl.ds(start, step)
            n = len(pieces)
            pieces.append(
                (
                    pltpu.make_async_copy(source.at[at], buf.at[at], in_sem.at[n]),
                    pltpu.make_async_copy(buf.at[at], target.at[at], out_sem.at[n]),
                )
            )
    for arrive, _ in pieces:
        arrive.start()
    for arrive, leave in pieces:
        arrive.wait()
        leave.start()
    for _, leave in pieces:
        leave.wait()


def on_device(
    leaf_n,
    vec_n,
    axes,
    points,
    probe_vectors,
    neighbours,
    leaf_pivots,
    leaf_inverse,
    local_pivots,
    local_inverse,
    upper_pivots,
    upper_inverse,
):
    group, columns, size = probe_vectors.shape
    rank = leaf_pivots.shape[1]
    slots = neighbours.shape[1]
    levels = group.bit_length() - 1
    total = columns * vec_n
    nodes = levels + UPL
    part = group // 2
    pivot_rows = max(p.shape[0] for p in (leaf_pivots, local_pivots, upper_pivots))
    maps = sum((group >> t) - 1 for t in range(levels))
    anywhere = pl.BlockSpec(memory_space=pl.ANY)
    hbm = pl.BlockSpec(memory_space=pltpu.HBM)
    dma = pltpu.SemaphoreType.DMA
    shapes = (
        jax.ShapeDtypeStruct((group, rank, size), F32),
        jax.ShapeDtypeStruct((group - 1, rank, 2 * rank), F32),
        jax.ShapeDtypeStruct((1, UPL, rank, 2 * rank), F32),
        jax.ShapeDtypeStruct((1, columns, rank), F32),
    )
    made = pl.pallas_call(
        functools.partial(body, leaf_n, vec_n, axes),
        out_shape=shapes,
        in_specs=[hbm] * 9,
        out_specs=[anywhere] * 4,
        scratch_shapes=[
            pltpu.SMEM((group, slots), jnp.int32),
            pltpu.VMEM((3, -(-pivot_rows // 8) * 8, rank), jnp.int32),
            pltpu.VMEM((3, 3, group, size), BF16),
            pltpu.VMEM((3 * group, 2 * columns, size), BF16),
            pltpu.VMEM((group, 16, size), BF16),
            pltpu.VMEM((3 * group, size, 16), BF16),
            pltpu.VMEM((part, slots * size, size), BF16),
            pltpu.VMEM((2 * columns, slots * size), BF16),
            pltpu.VMEM((nodes + 1, rank, rank), F32),
            pltpu.VMEM((nodes + 1, 2, rank, size), BF16),
            pltpu.VMEM((part - 1, 2 * columns, size), F32),
            pltpu.VMEM((total, size), F32),
            pltpu.VMEM((nodes, 2, rank, total), F32),
            pltpu.VMEM((total, 2 * rank), F32),
            pltpu.VMEM((rank, size), F32),
            pltpu.VMEM((nodes, rank, 2 * rank), F32),
            pltpu.VMEM((1, columns, rank), F32),
            dma((nodes + 1,)),
            dma((3,)),
            dma((3,)),
            dma((7,)),
            dma((7,)),
            dma((part - 1,)),
            dma((part - 1,)),
            dma((nodes,)),
            dma((nodes,)),
            dma((maps,)),
            dma((maps,)),
            dma((nodes + 2,)),
        ],
        compiler_params=pltpu.CompilerParams(
            collective_id=0, has_side_effects=True, vmem_limit_bytes=60 * 2**20
        ),
    )(
        jnp.transpose(points, (1, 0, 2)),
        probe_vectors,
        neighbours,
        leaf_pivots,
        leaf_inverse,
        local_pivots,
        local_inverse,
        upper_pivots,
        upper_inverse,
    )
    leaf_map, local_map, upper_map, top = pl.pallas_call(
        write_out,
        out_shape=shapes,
        in_specs=[anywhere] * 4,
        out_specs=[hbm] * 4,
        scratch_shapes=[pltpu.VMEM(p.shape, p.dtype) for p in shapes] + [dma((9,))] * 2,
        compiler_params=pltpu.CompilerParams(vmem_limit_bytes=60 * 2**20),
    )(*made)
    return (
        jnp.swapaxes(leaf_map, 1, 2),
        jnp.swapaxes(local_map, 1, 2),
        jnp.swapaxes(upper_map, 2, 3),
        top,
    )


def solution(mesh):
    axes = tuple(mesh.axis_names)
    placed = (
        P("leaf", None, None),
        P("leaf", "vec", None),
        P("leaf", None),
        P("leaf", None),
        P("leaf", None, None),
        P("leaf", None),
        P("leaf", None, None),
        P(),
        P(),
    )
    return jax.shard_map(
        functools.partial(on_device, mesh.shape["leaf"], mesh.shape["vec"], axes),
        mesh=mesh,
        in_specs=placed,
        out_specs=(
            P("leaf", None, None),
            P("leaf", None, None),
            P("leaf", None, None, None),
            P("leaf", "vec", None),
        ),
        check_vma=False,
    )
```

time: 104 us -> 65.2 us (0.63)
  the two profiles are of different devices: /device:TPU:1 before, /device:TPU:106 now
where the time goes in v2:
time: 65.2 us; the launch traced here: 65.1 us
  Pallas kernels  64.4 us (99%)
    pallas_call x1, Pallas kernels, on_device(): pl.pallas_call(functools.partial(body, leaf_n, vec_n, axes), out_shape=sh...  62.2 us
    pallas_call x1, Pallas kernels, on_device(): pl.pallas_call(write_out, out_shape=shapes, in_specs=[anywhere] * 4, out_...  2.26 us

profile of v2, /device:TPU:106, one launch (start us, length us, event | category | flops | bytes accessed | tf_op | source)
XLA Modules:
  0.0 65.1 jit_solution(552269751099606505)
XLA Ops:
  0.6 62.2 %shard_map.120 = (f32[16,64,256]{2,1,0:T(8,128)}, f32[15,64,128]{2,1,0:T(8,128)}, f32[1,3,64,128]{3,2,1,0:T(8,128)}, f32[1,16,64]{2,1,0:T(8,128)}) custom-call(bf16[3,16,256]{2,1,0:T(8,128)(2,1)} %bitcast.4, bf16[16,16,256]{2,1,0:T(8,128)(2,1)} %probe.1, s32[16,16]{1,0:T(8,128)} %nbr_in.1, s32[16,64]{1,0:T(8,128)} %leaf_piv.1, f32[16,64,64]{2,1,0:T(8,128)} %leaf_inv.1, ...), custom_call_target="tpu_custom_call" | custom-call | tf_op jit(solution)/shard_map/pallas_call | solution.py:472
  62.8 2.3 %shard_map.121 = (f32[16,64,256]{2,1,0:T(8,128)}, f32[15,64,128]{2,1,0:T(8,128)}, f32[1,3,64,128]{3,2,1,0:T(8,128)}, f32[1,16,64]{2,1,0:T(8,128)}) custom-call(f32[16,64,256]{2,1,0:T(8,128)} %get-tuple-element.12.a, f32[15,64,128]{2,1,0:T(8,128)} %get-tuple-element.13.b, f32[1,3,64,128]{3,2,1,0:T(8,128)} %get-tuple-element.14.c, ...), custom_call_target="tpu_custom_call" | custom-call | tf_op jit(solution)/shard_map/pallas_call | solution.py:522

commit v3 on v2

v3 whole, which is shorter than its diff:
```python
import functools

import jax
import jax.numpy as jnp
from jax import lax
from jax.experimental import pallas as pl
from jax.experimental.pallas import tpu as pltpu
from jax.sharding import PartitionSpec as P

UPL = 3
SOFTEN = 0.0009
EPSILON = 1e-06
F32 = jnp.float32
BF16 = jnp.bfloat16
NN = (((1,), (0,)), ((), ()))
NT = (((1,), (1,)), ((), ()))


def mm(a, b, dims=NN):
    return lax.dot_general(a, b, dims, preferred_element_type=F32)


def split(a):
    high = a.astype(BF16)
    return high, (a - high.astype(F32)).astype(BF16)


def mm3(a, b, dims=NN):
    return mm(a[0], b[0], dims) + (mm(a[0], b[1], dims) + mm(a[1], b[0], dims))


def feature_rows(xyz, weight):
    norm = SOFTEN / 2 + xyz[0] * xyz[0] + xyz[1] * xyz[1] + xyz[2] * xyz[2]
    high = norm.astype(BF16).astype(F32)
    rest = norm - high
    middle = rest.astype(BF16).astype(F32)
    low = (rest - middle).astype(BF16).astype(F32)
    return [part * weight for part in (high, middle, low)]


def body(
    leaf_n,
    vec_n,
    axes,
    pts,
    probe,
    nbr_in,
    leaf_piv,
    leaf_inv,
    local_piv,
    local_inv,
    upper_piv,
    upper_inv,
    out_leaf,
    out_local,
    out_upper,
    out_top,
    nbr,
    piv,
    ext_pts,
    ext_probe,
    near,
    far,
    tiles,
    vectors,
    inv,
    weights,
    upper_weights,
    sketches,
    z_ref,
    quad,
    twin,
    joined,
    z_top,
    leaf_map,
    maps,
    upper_maps,
    top_ref,
    inv_sem,
    piv_sem,
    own_sem,
    side_send,
    side_recv,
    sk_send,
    sk_recv,
    ex_send,
    ex_recv,
    mate_send,
    mate_recv,
    map_send,
    map_recv,
    out_sem,
):
    leaf_axis, vec_axis = axes
    d = lax.axis_index(leaf_axis)
    v = lax.axis_index(vec_axis)
    group, columns, points = probe.shape
    rank = inv.shape[1]
    total = columns * vec_n
    wide = 2 * columns
    slots = nbr.shape[1]
    part = group // 2

    x, y = v % 4, v // 4
    pair, side_row = x // 2, x % 2
    half = ((x + 1) // 2) % 2
    w = part * half + 4 * pair + y
    own = w % part
    core = d % 2
    lead = core == 1

    def vec_of(cluster):
        high, low = cluster // part, (cluster // 4) % 2
        return 4 * (cluster % 4) + 2 * low + (high + low) % 2

    def on_vec(u):
        return {leaf_axis: d, vec_axis: u}

    def on_leaf(g):
        return {leaf_axis: g, vec_axis: v}

    def remote(src, dst, send, recv, target):
        return pltpu.make_async_remote_copy(
            src_ref=src,
            dst_ref=dst,
            send_sem=send,
            recv_sem=recv,
            device_id=target,
            device_id_type=pl.DeviceIdType.MESH,
        )

    def flip(index, stride):
        return index + stride * (1 - 2 * ((index // stride) % 2))

    before = (d + leaf_n - 1) % leaf_n
    after = (d + 1) % leaf_n
    mate = flip(d, 1)
    lead_row = d - core + 1

    barrier = pltpu.get_barrier_semaphore()
    targets = [on_vec((v + t) % vec_n) for t in range(1, vec_n)]
    targets += [on_leaf(g) for g in (before, after, flip(d, 2), flip(d, 4))]
    targets += [
        {leaf_axis: mate, vec_axis: vec_of(half * part + (own + t) % part)}
        for t in range(1, part)
    ]
    for target in targets:
        pl.semaphore_signal(
            barrier, inc=1, device_id=target, device_id_type=pl.DeviceIdType.MESH
        )

    mine = [
        pltpu.make_async_copy(pts, ext_pts.at[1], own_sem.at[0]),
        pltpu.make_async_copy(nbr_in, nbr, own_sem.at[1]),
        pltpu.make_async_copy(
            probe,
            ext_probe.at[
                pl.ds(group, group),
                pl.ds(pl.multiple_of(columns * side_row, columns), columns),
            ],
            own_sem.at[2],
        ),
    ]
    quarter = w // 4
    rows = [(0, leaf_inv, w)]
    rows += [(1, local_inv, 2 * quarter + n) for n in range(2)]
    rows += [(1, local_inv, group // 2 + quarter)]
    rows += [(1, local_inv, group - 4 + n) for n in range(3)]
    local_nodes = len(rows)
    offset = 0
    for u in range(1, UPL + 1):
        rows.append((2, upper_inv, offset + d // (1 << u)))
        offset += leaf_n >> u
    inv_copies = [
        pltpu.make_async_copy(source.at[row], inv.at[n], inv_sem.at[n])
        for n, (_, source, row) in enumerate(rows)
    ]
    piv_copies = [
        pltpu.make_async_copy(
            source, piv.at[n, pl.ds(0, source.shape[0])], piv_sem.at[n]
        )
        for n, source in enumerate((leaf_piv, local_piv, upper_piv))
    ]
    for copy in mine[:1] + piv_copies + inv_copies + mine[1:]:
        copy.start()

    def features(side):
        xyz = [ext_pts[side, c].astype(F32) for c in range(3)]
        norm = feature_rows(xyz, 4096.0)
        one = jnp.ones((1, points), F32)
        pad = jnp.zeros((7, points), F32)
        for r in range(group):
            at = [q[r : r + 1] for q in xyz]
            nm = [q[r : r + 1] for q in norm]
            if side == 1:
                near[r] = jnp.concatenate(at + nm + [one] * 3 + [pad], axis=0).astype(BF16)
            rows_far = [q * -8192.0 for q in at] + [one] * 3 + nm + [pad]
            far[side * group + r] = jnp.transpose(
                jnp.concatenate(rows_far, axis=0)
            ).astype(BF16)

    mine[0].wait()
    features(1)

    for copy in piv_copies:
        copy.wait()
    for n, (which, _, row) in enumerate(rows):
        inv_copies[n].wait()
        size = points if n == 0 else 2 * rank
        chosen = piv[which, pl.ds(row, 1), :]
        spread = (
            lax.broadcasted_iota(jnp.int32, (size, rank), 0) == chosen
        ).astype(F32).astype(BF16)
        for m, piece in enumerate(split(jnp.transpose(inv[n]))):
            scattered = mm(piece, spread, NT).astype(BF16)
            if n < local_nodes:
                weights[core, n, m, :, :size] = scattered
            else:
                upper_weights[n - local_nodes, m] = scattered
    mine[1].wait()
    mine[2].wait()

    pl.semaphore_wait(barrier, len(targets))

    def strip(place, row, piece=None):
        start, count = place * group, group
        if piece is not None:
            start, count = start + piece * part, part
        return ext_probe.at[
            pl.ds(start, count), pl.ds(pl.multiple_of(columns * row, columns), columns)
        ]

    ways = [(after, 0), (before, 2)]
    pts_copies = [
        remote(pts, ext_pts.at[place], side_send.at[n], side_recv.at[n], on_leaf(target))
        for n, (target, place) in enumerate(ways)
    ]
    pair_copies = [
        remote(
            probe.at[pl.ds(piece * part, part)],
            strip(1, side_row, piece),
            side_send.at[2 + piece],
            side_recv.at[2 + piece],
            on_vec(flip(v, 1)),
        )
        for piece in range(2)
    ]
    direct = [
        remote(
            probe,
            strip(place, side_row),
            side_send.at[4 + n],
            side_recv.at[4 + n],
            on_leaf(target),
        )
        for n, (target, place) in enumerate(ways)
    ]

    def passed(piece):
        return [
            remote(
                strip(1, 1 - side_row, piece),
                strip(place, 1 - side_row, piece),
                side_send.at[6 + 2 * piece + n],
                side_recv.at[6 + 2 * piece + n],
                on_leaf(target),
            )
            for n, (target, place) in enumerate(ways)
        ]

    for copy in pts_copies + pair_copies + direct:
        copy.start()

    def hand(n, src, dst):
        return remote(src, dst, mate_send.at[n], mate_recv.at[n], on_leaf(mate))

    give_weights = hand(0, weights.at[0], weights.at[0])

    @pl.when(core == 0)
    def _():
        give_weights.start()

    pts_copies[0].wait_recv()
    features(0)
    pts_copies[1].wait_recv()
    features(2)

    first = (d - 1) * group

    def place_of(c, k):
        listed = nbr[c, k]
        return jnp.clip(listed - first, 0, 3 * group - 1), listed >= 0

    @pl.loop(0, part)
    def _(c):
        cluster = half * part + c
        near_c = near[cluster]
        for k in range(slots):
            place, _ = place_of(cluster, k)
            tiles[c, k * points : (k + 1) * points, :] = lax.rsqrt(
                mm(far[place], near_c)
            ).astype(BF16)
        for piece in range(2):

            @pl.when(c == 2 * piece)
            def _():
                pair_copies[piece].wait_recv()
                for copy in passed(piece):
                    copy.start()

    for copy in direct + passed(0) + passed(1):
        copy.wait_recv()

    z_rows = pl.ds(pl.multiple_of(wide * (2 * y + pair), wide), wide)

    def sketch_copy(t, origin):
        c = half * part + (own + 1 + t) % part
        return remote(
            sketches.at[t],
            z_ref.at[origin, z_rows],
            sk_send.at[t],
            sk_recv.at[origin, t],
            {leaf_axis: lead_row, vec_axis: vec_of(c)},
        )

    last = hand(1, sketches.at[part - 1], z_ref.at[0, z_rows])

    @pl.loop(0, part)
    def _(t):
        c = (own + 1 + t) % part
        for k in range(slots):
            place, listed = place_of(half * part + c, k)
            block = ext_probe[place]
            vectors[:, k * points : (k + 1) * points] = jnp.where(
                listed, block, jnp.zeros_like(block)
            )
        sketches[t] = mm(vectors[...], tiles[c])

        @pl.when(t < part - 1)
        def _():
            sketch_copy(t, core).start()

    place_a = pl.ds(2 * quarter, 2)

    def publish_leaf():
        copies = [pltpu.make_async_copy(leaf_map.at[core], out_leaf.at[w], out_sem.at[0])]
        for j in range(1, group):
            copies.append(
                remote(
                    leaf_map.at[core],
                    out_leaf.at[w],
                    map_send.at[j - 1],
                    map_recv.at[j - 1],
                    on_vec(vec_of((w + j) % group)),
                )
            )
        return copies

    def publish_local():
        blocks = [
            (maps.at[core, pl.ds(0, 2)], out_local.at[place_a]),
            (maps.at[core, 2], out_local.at[group // 2 + quarter]),
        ]
        copies = [
            pltpu.make_async_copy(src, dst, out_sem.at[1 + n])
            for n, (src, dst) in enumerate(blocks)
        ]
        for j in range(1, 4):
            target = on_vec(vec_of((w + 4 * j) % group))
            for n, (src, dst) in enumerate(blocks):
                m = group - 1 + 2 * (j - 1) + n
                copies.append(remote(src, dst, map_send.at[m], map_recv.at[m], target))
        return copies

    give_leaf = hand(2, leaf_map.at[0], leaf_map.at[0])
    give_a = hand(3, maps.at[0, pl.ds(0, 3)], maps.at[0, pl.ds(0, 3)])
    top_rows = pl.ds(group - 4, 3)
    give_b = hand(4, maps.at[0, pl.ds(3, 3)], out_local.at[top_rows])
    give_upper = [
        hand(5 + u, upper_maps.at[u], out_upper.at[0, u]) for u in range(UPL)
    ]
    give_top = hand(5 + UPL, top_ref, out_top)
    gifts = [give_b] + give_upper + [give_top]

    def peer(r, k):
        pos = w % 4 if r == 0 else quarter
        other = flip(pos, k) if k < 3 else 3 - pos
        cluster = 4 * quarter + other if r == 0 else 4 * other + w % 4
        return pos, on_vec(vec_of(cluster))

    def round_copy(r, k):
        pos, target = peer(r, k)
        return remote(
            quad.at[r, pos],
            quad.at[r, pos],
            ex_send.at[3 * r + k - 1],
            ex_recv.at[3 * r + k - 1],
            target,
        )

    def upper_copy(u):
        branch = (d // (1 << u)) % 2
        return remote(
            joined.at[u - 1, branch],
            joined.at[u - 1, branch],
            ex_send.at[5 + u],
            ex_recv.at[5 + u],
            on_leaf(flip(d, 1 << u)),
        )

    def node(scattered, z, zt):
        size = zt.shape[0]
        z_parts, zt_parts = split(z), split(zt)
        mean_sq = jnp.sum(z * z) / (size * total) + EPSILON
        gram = split(mm3(zt_parts, z_parts))
        interp = mm3(scattered, gram) / (total * mean_sq)
        return interp, mean_sq, zt_parts

    def up_of(interp, mean_sq, zt_parts):
        return mm3(split(interp), zt_parts) * lax.rsqrt(mean_sq)

    def join(left, right):
        zt = jnp.concatenate([left, right], axis=0)
        return jnp.transpose(zt), zt

    def local_weights(g, n):
        return weights[g, n, 0, :, : 2 * rank], weights[g, n, 1, :, : 2 * rank]

    @pl.when(core == 0)
    def _():
        last.start()
        give_leaf.wait_recv()
        for copy in publish_leaf():
            copy.start()
        give_a.wait_recv()
        for copy in publish_local():
            copy.start()
        for copy in gifts:
            copy.wait_recv()
        give_weights.wait_send()
        last.wait_send()

    @pl.when(lead)
    def _():
        z_ref[1, z_rows, :] = sketches[part - 1]
        give_weights.wait_recv()

        @pl.loop(0, part - 1)
        def _(t):
            sketch_copy(t, 1).wait_recv()
            sketch_copy(t, 0).wait_recv()

        last.wait_recv()
        pos = w % 4
        for g in range(2):
            z = z_ref[g]
            made = node((weights[g, 0, 0], weights[g, 0, 1]), z, jnp.transpose(z))
            leaf_map[g] = made[0]
            quad[0, pos, g] = up_of(*made)
        for r in range(2):
            pos = w % 4 if r == 0 else quarter
            branch = pos // 2
            for k in (1, 3, 2):
                round_copy(r, k).start()
            if r == 1:
                give_leaf.start()
                give_a.start()
                for copy in publish_leaf() + publish_local():
                    copy.start()
            for which, side in ((0, branch), (1, 1 - branch)):
                for k in ((1,), (2, 3))[which]:
                    round_copy(r, k).wait_recv()
                for g in range(2):
                    z, zt = join(quad[r, 2 * side, g], quad[r, 2 * side + 1, g])
                    made = node(local_weights(g, 1 + 3 * r + side), z, zt)
                    maps[g, 3 * r + side] = made[0]
                    twin[r, side, g] = up_of(*made)
            for g in range(2):
                z, zt = join(twin[r, 0, g], twin[r, 1, g])
                made = node(local_weights(g, 3 + 3 * r), z, zt)
                maps[g, 3 * r + 2] = made[0]
                if r == 0:
                    quad[1, quarter, g] = up_of(*made)
                else:
                    twin[2, 0, g] = up_of(*made)
        give_b.start()
        own_b = pltpu.make_async_copy(
            maps.at[1, pl.ds(3, 3)], out_local.at[top_rows], out_sem.at[3]
        )
        own_b.start()
        z, zt = join(twin[2, 0, 0], twin[2, 0, 1])
        own_upper = []
        for u in range(UPL):
            made = node((upper_weights[u, 0], upper_weights[u, 1]), z, zt)
            upper_maps[u] = made[0]
            if u + 1 < UPL:
                joined[u, (d // (2 << u)) % 2] = up_of(*made)
                upper_copy(u + 1).start()
            give_upper[u].start()
            own_upper.append(
                pltpu.make_async_copy(
                    upper_maps.at[u], out_upper.at[0, u], out_sem.at[4 + u]
                )
            )
            own_upper[-1].start()
            if u + 1 < UPL:
                upper_copy(u + 1).wait_recv()
                z, zt = join(joined[u, 0], joined[u, 1])
            else:
                z_top[...] = z
                kept = z_top[pl.ds(pl.multiple_of(v * columns, columns), columns), :]
                top_ref[0] = mm3(split(kept), split(made[0]), NT) * lax.rsqrt(made[1])
        give_top.start()
        own_top = pltpu.make_async_copy(top_ref, out_top, out_sem.at[4 + UPL])
        own_top.start()
        for copy in [own_b, own_top] + own_upper:
            copy.wait()
        for copy in [give_leaf, give_a] + gifts:
            copy.wait_send()
        for r in range(2):
            for k in range(1, 4):
                round_copy(r, k).wait_send()
        for u in range(1, UPL):
            upper_copy(u).wait_send()

    @pl.loop(0, part - 1)
    def _(t):
        sketch_copy(t, core).wait_send()

    for copy in pts_copies + pair_copies + direct + passed(0) + passed(1):
        copy.wait_send()
    for copy in publish_leaf() + publish_local():
        copy.wait()


def write_out(a, b, c, e, out_a, out_b, out_c, out_e, buf_a, buf_b, buf_c, buf_e, in_sem, out_sem):
    pieces = []
    for source, buf, target, step in (
        (a, buf_a, out_a, 4),
        (b, buf_b, out_b, 5),
        (c, buf_c, out_c, 1),
        (e, buf_e, out_e, 1),
    ):
        for start in range(0, source.shape[0], step):
            at = pl.ds(start, step)
            n = len(pieces)
            pieces.append(
                (
                    pltpu.make_async_copy(source.at[at], buf.at[at], in_sem.at[n]),
                    pltpu.make_async_copy(buf.at[at], target.at[at], out_sem.at[n]),
                )
            )
    for arrive, _ in pieces:
        arrive.start()
    for arrive, leave in pieces:
        arrive.wait()
        leave.start()
    for _, leave in pieces:
        leave.wait()


def on_device(
    leaf_n,
    vec_n,
    axes,
    points,
    probe_vectors,
    neighbours,
    leaf_pivots,
    leaf_inverse,
    local_pivots,
    local_inverse,
    upper_pivots,
    upper_inverse,
):
    group, columns, size = probe_vectors.shape
    rank = leaf_pivots.shape[1]
    slots = neighbours.shape[1]
    total = columns * vec_n
    part = group // 2
    pivot_rows = max(p.shape[0] for p in (leaf_pivots, local_pivots, upper_pivots))
    anywhere = pl.BlockSpec(memory_space=pl.ANY)
    hbm = pl.BlockSpec(memory_space=pltpu.HBM)
    dma = pltpu.SemaphoreType.DMA
    shapes = (
        jax.ShapeDtypeStruct((group, rank, size), F32),
        jax.ShapeDtypeStruct((group - 1, rank, 2 * rank), F32),
        jax.ShapeDtypeStruct((1, UPL, rank, 2 * rank), F32),
        jax.ShapeDtypeStruct((1, columns, rank), F32),
    )
    made = pl.pallas_call(
        functools.partial(body, leaf_n, vec_n, axes),
        out_shape=shapes,
        in_specs=[hbm] * 9,
        out_specs=[anywhere] * 4,
        scratch_shapes=[
            pltpu.SMEM((group, slots), jnp.int32),
            pltpu.VMEM((3, -(-pivot_rows // 8) * 8, rank), jnp.int32),
            pltpu.VMEM((3, 3, group, size), BF16),
            pltpu.VMEM((3 * group, 2 * columns, size), BF16),
            pltpu.VMEM((group, 16, size), BF16),
            pltpu.VMEM((3 * group, size, 16), BF16),
            pltpu.VMEM((part, slots * size, size), BF16),
            pltpu.VMEM((2 * columns, slots * size), BF16),
            pltpu.VMEM((7 + UPL, rank, rank), F32),
            pltpu.VMEM((2, 7, 2, rank, size), BF16),
            pltpu.VMEM((UPL, 2, rank, 2 * rank), BF16),
            pltpu.VMEM((part, 2 * columns, size), F32),
            pltpu.VMEM((2, total, size), F32),
            pltpu.VMEM((2, 4, 2, rank, total), F32),
            pltpu.VMEM((3, 2, 2, rank, total), F32),
            pltpu.VMEM((UPL - 1, 2, rank, total), F32),
            pltpu.VMEM((total, 2 * rank), F32),
            pltpu.VMEM((2, rank, size), F32),
            pltpu.VMEM((2, 6, rank, 2 * rank), F32),
            pltpu.VMEM((UPL, rank, 2 * rank), F32),
            pltpu.VMEM((1, columns, rank), F32),
            dma((7 + UPL,)),
            dma((3,)),
            dma((3,)),
            dma((10,)),
            dma((10,)),
            dma((part,)),
            dma((2, part)),
            dma((6 + UPL,)),
            dma((6 + UPL,)),
            dma((6 + UPL,)),
            dma((6 + UPL,)),
            dma((group + 5,)),
            dma((group + 5,)),
            dma((5 + UPL,)),
        ],
        compiler_params=pltpu.CompilerParams(
            collective_id=0, has_side_effects=True, vmem_limit_bytes=60 * 2**20
        ),
    )(
        jnp.transpose(points, (1, 0, 2)),
        probe_vectors,
        neighbours,
        leaf_pivots,
        leaf_inverse,
        local_pivots,
        local_inverse,
        upper_pivots,
        upper_inverse,
    )
    leaf_map, local_map, upper_map, top = pl.pallas_call(
        write_out,
        out_shape=shapes,
        in_specs=[anywhere] * 4,
        out_specs=[hbm] * 4,
        scratch_shapes=[pltpu.VMEM(p.shape, p.dtype) for p in shapes] + [dma((9,))] * 2,
        compiler_params=pltpu.CompilerParams(vmem_limit_bytes=60 * 2**20),
    )(*made)
    return (
        jnp.swapaxes(leaf_map, 1, 2),
        jnp.swapaxes(local_map, 1, 2),
        jnp.swapaxes(upper_map, 2, 3),
        top,
    )


def solution(mesh):
    axes = tuple(mesh.axis_names)
    placed = (
        P("leaf", None, None),
        P("leaf", "vec", None),
        P("leaf", None),
        P("leaf", None),
        P("leaf", None, None),
        P("leaf", None),
        P("leaf", None, None),
        P(),
        P(),
    )
    return jax.shard_map(
        functools.partial(on_device, mesh.shape["leaf"], mesh.shape["vec"], axes),
        mesh=mesh,
        in_specs=placed,
        out_specs=(
            P("leaf", None, None),
            P("leaf", None, None),
            P("leaf", None, None, None),
            P("leaf", "vec", None),
        ),
        check_vma=False,
    )
```

time: 65.2 us -> 65.1 us (level)
  the two profiles are of different devices: /device:TPU:106 before, /device:TPU:1 now
where the time goes in v3:
time: 65.1 us; the launch traced here: 64.9 us
  Pallas kernels  64.3 us (99%)
    pallas_call x1, Pallas kernels, on_device(): pl.pallas_call(functools.partial(body, leaf_n, vec_n, axes), out_shape=sh...  62 us
    pallas_call x1, Pallas kernels, on_device(): pl.pallas_call(write_out, out_shape=shapes, in_specs=[anywhere] * 4, out_...  2.26 us

profile of v3, /device:TPU:1, one launch (start us, length us, event | category | flops | bytes accessed | tf_op | source)
XLA Modules:
  0.0 64.9 jit_solution(15105931006365851344)
XLA Ops:
  0.6 62.0 %shard_map.120 = (f32[16,64,256]{2,1,0:T(8,128)}, f32[15,64,128]{2,1,0:T(8,128)}, f32[1,3,64,128]{3,2,1,0:T(8,128)}, f32[1,16,64]{2,1,0:T(8,128)}) custom-call(bf16[3,16,256]{2,1,0:T(8,128)(2,1)} %bitcast.4, bf16[16,16,256]{2,1,0:T(8,128)(2,1)} %probe.1, s32[16,16]{1,0:T(8,128)} %nbr_in.1, s32[16,64]{1,0:T(8,128)} %leaf_piv.1, f32[16,64,64]{2,1,0:T(8,128)} %leaf_inv.1, ...), custom_call_target="tpu_custom_call" | custom-call | tf_op jit(solution)/shard_map/pallas_call | solution.py:591
  62.7 2.3 %shard_map.121 = (f32[16,64,256]{2,1,0:T(8,128)}, f32[15,64,128]{2,1,0:T(8,128)}, f32[1,3,64,128]{3,2,1,0:T(8,128)}, f32[1,16,64]{2,1,0:T(8,128)}) custom-call(f32[16,64,256]{2,1,0:T(8,128)} %get-tuple-element.12.a, f32[15,64,128]{2,1,0:T(8,128)} %get-tuple-element.13.b, f32[1,3,64,128]{3,2,1,0:T(8,128)} %get-tuple-element.14.c, ...), custom_call_target="tpu_custom_call" | custom-call | tf_op jit(solution)/shard_map/pallas_call | solution.py:647

commit v4 on v3

--- a/solution.py
+++ b/solution.py
@@ -73,6 +73,8 @@
     joined,
     z_top,
     leaf_map,
+    all_leaf,
+    all_local,
     maps,
     upper_maps,
     top_ref,
@@ -340,47 +342,86 @@
         def _():
             sketch_copy(t, core).start()
 
-    place_a = pl.ds(2 * quarter, 2)
-
-    def publish_leaf():
-        copies = [pltpu.make_async_copy(leaf_map.at[core], out_leaf.at[w], out_sem.at[0])]
-        for j in range(1, group):
-            copies.append(
-                remote(
-                    leaf_map.at[core],
-                    out_leaf.at[w],
-                    map_send.at[j - 1],
-                    map_recv.at[j - 1],
-                    on_vec(vec_of((w + j) % group)),
-                )
-            )
-        return copies
-
-    def publish_local():
-        blocks = [
-            (maps.at[core, pl.ds(0, 2)], out_local.at[place_a]),
-            (maps.at[core, 2], out_local.at[group // 2 + quarter]),
-        ]
-        copies = [
-            pltpu.make_async_copy(src, dst, out_sem.at[1 + n])
-            for n, (src, dst) in enumerate(blocks)
-        ]
-        for j in range(1, 4):
-            target = on_vec(vec_of((w + 4 * j) % group))
-            for n, (src, dst) in enumerate(blocks):
-                m = group - 1 + 2 * (j - 1) + n
-                copies.append(remote(src, dst, map_send.at[m], map_recv.at[m], target))
-        return copies
-
-    give_leaf = hand(2, leaf_map.at[0], leaf_map.at[0])
-    give_a = hand(3, maps.at[0, pl.ds(0, 3)], maps.at[0, pl.ds(0, 3)])
+    def column(q):
+        return 2 * (((q + 1) // 2) % 2) + q // 2
+
+    def along(sem, src, dst, step_x, step_y):
+        return remote(
+            src,
+            dst,
+            map_send.at[sem],
+            map_recv.at[sem],
+            on_vec(4 * ((y + step_y) % 4) + (x + step_x) % 4),
+        )
+
+    def same(sem, ref, step_x, step_y):
+        return along(sem, ref, ref, step_x, step_y)
+
+    steps = (1, 3)
+    order = (0, 3, 1, 2)
+
+    def full_x(way, o):
+        return same(
+            4 * way + o, all_leaf.at[x, :, (y + order[o]) % 4], steps[way], 0
+        )
+
+    def half_x(way, o):
+        source = (x + 4 - steps[way]) % 4
+        return same(
+            8 + 4 * way + o,
+            all_leaf.at[source, way, (y + order[o]) % 4],
+            steps[way],
+            0,
+        )
+
+    def full_y(way):
+        return same(16 + way, all_leaf.at[x, :, y], 0, steps[way])
+
+    def half_y(way):
+        source = (y + 4 - steps[way]) % 4
+        return same(18 + way, all_leaf.at[x, way, source], 0, steps[way])
+
+    def local_rows(q, n):
+        return pl.ds(2 * column(q), 2) if n == 0 else pl.ds(group // 2 + column(q), 1)
+
+    def full_local(way, n):
+        return same(20 + 2 * way + n, all_local.at[:, local_rows(x, n)], steps[way], 0)
+
+    def half_local(way, n):
+        source = (x + 4 - steps[way]) % 4
+        return same(
+            24 + 2 * way + n, all_local.at[way, local_rows(source, n)], steps[way], 0
+        )
+
+    give_leaf = hand(2, leaf_map, all_leaf.at[x, :, y])
+    give_a = [
+        hand(3 + n, maps.at[:, rows_of], all_local.at[:, local_rows(x, n)])
+        for n, rows_of in enumerate((pl.ds(0, 2), pl.ds(2, 1)))
+    ]
     top_rows = pl.ds(group - 4, 3)
-    give_b = hand(4, maps.at[0, pl.ds(3, 3)], out_local.at[top_rows])
+    give_b = hand(5, maps.at[0, pl.ds(3, 3)], out_local.at[top_rows])
     give_upper = [
-        hand(5 + u, upper_maps.at[u], out_upper.at[0, u]) for u in range(UPL)
-    ]
-    give_top = hand(5 + UPL, top_ref, out_top)
+        hand(6 + u, upper_maps.at[u], out_upper.at[0, u]) for u in range(UPL)
+    ]
+    give_top = hand(6 + UPL, top_ref, out_top)
     gifts = [give_b] + give_upper + [give_top]
+    low_rows = pl.ds(0, group - 4)
+
+    def leaf_columns(n):
+        q = (x + n) % 4
+        at = pl.ds(4 * column(q), 4)
+        return (
+            pltpu.make_async_copy(all_leaf.at[q, 0], out_leaf.at[at], out_sem.at[n]),
+            hand(7 + UPL + n, all_leaf.at[q, 1], out_leaf.at[at]),
+        )
+
+    def low_levels():
+        return (
+            pltpu.make_async_copy(
+                all_local.at[0], out_local.at[low_rows], out_sem.at[4]
+            ),
+            hand(11 + UPL, all_local.at[1], out_local.at[low_rows]),
+        )
 
     def peer(r, k):
         pos = w % 4 if r == 0 else quarter
@@ -430,11 +471,64 @@
     def _():
         last.start()
         give_leaf.wait_recv()
-        for copy in publish_leaf():
+        for way in range(2):
+            full_y(way).start()
+        for way in range(2):
+            full_x(way, 0).start()
+        for came in range(2):
+            full_y(came).wait_recv()
+            half_y(came).start()
+            for way in range(2):
+                full_x(way, 1 + came).start()
+        for way in range(2):
+            full_x(way, 0).wait_recv()
+            half_x(way, 0).start()
+        for way in range(2):
+            half_y(way).wait_recv()
+        for way in range(2):
+            full_x(way, 3).start()
+        for copy in leaf_columns(0):
             copy.start()
-        give_a.wait_recv()
-        for copy in publish_local():
+        for o in (1, 2):
+            for way in range(2):
+                full_x(way, o).wait_recv()
+                half_x(way, o).start()
+        for copy in give_a:
+            copy.wait_recv()
+        for way in range(2):
+            for n in range(2):
+                full_local(way, n).start()
+        for way in range(2):
+            full_x(way, 3).wait_recv()
+            half_x(way, 3).start()
+        for copy in leaf_columns(1) + leaf_columns(3):
             copy.start()
+        for way in range(2):
+            for n in range(2):
+                full_local(way, n).wait_recv()
+                half_local(way, n).start()
+        for o in range(4):
+            for way in range(2):
+                half_x(way, o).wait_recv()
+        for copy in leaf_columns(2):
+            copy.start()
+        for way in range(2):
+            for n in range(2):
+                half_local(way, n).wait_recv()
+        for copy in low_levels():
+            copy.start()
+        for way in range(2):
+            full_y(way).wait_send()
+            half_y(way).wait_send()
+            for o in range(4):
+                full_x(way, o).wait_send()
+                half_x(way, o).wait_send()
+            for n in range(2):
+                full_local(way, n).wait_send()
+                half_local(way, n).wait_send()
+        for local, across in [leaf_columns(n) for n in range(4)] + [low_levels()]:
+            local.wait()
+            across.wait_send()
         for copy in gifts:
             copy.wait_recv()
         give_weights.wait_send()
@@ -462,11 +556,8 @@
             branch = pos // 2
             for k in (1, 3, 2):
                 round_copy(r, k).start()
-            if r == 1:
-                give_leaf.start()
-                give_a.start()
-                for copy in publish_leaf() + publish_local():
-                    copy.start()
+            for copy in (give_a if r else [give_leaf]):
+                copy.start()
             for which, side in ((0, branch), (1, 1 - branch)):
                 for k in ((1,), (2, 3))[which]:
                     round_copy(r, k).wait_recv()
@@ -485,7 +576,7 @@
                     twin[2, 0, g] = up_of(*made)
         give_b.start()
         own_b = pltpu.make_async_copy(
-            maps.at[1, pl.ds(3, 3)], out_local.at[top_rows], out_sem.at[3]
+            maps.at[1, pl.ds(3, 3)], out_local.at[top_rows], out_sem.at[0]
         )
         own_b.start()
         z, zt = join(twin[2, 0, 0], twin[2, 0, 1])
@@ -499,7 +590,7 @@
             give_upper[u].start()
             own_upper.append(
                 pltpu.make_async_copy(
-                    upper_maps.at[u], out_upper.at[0, u], out_sem.at[4 + u]
+                    upper_maps.at[u], out_upper.at[0, u], out_sem.at[1 + u]
                 )
             )
             own_upper[-1].start()
@@ -511,17 +602,19 @@
                 kept = z_top[pl.ds(pl.multiple_of(v * columns, columns), columns), :]
                 top_ref[0] = mm3(split(kept), split(made[0]), NT) * lax.rsqrt(made[1])
         give_top.start()
-        own_top = pltpu.make_async_copy(top_ref, out_top, out_sem.at[4 + UPL])
+        own_top = pltpu.make_async_copy(top_ref, out_top, out_sem.at[1 + UPL])
         own_top.start()
         for copy in [own_b, own_top] + own_upper:
             copy.wait()
-        for copy in [give_leaf, give_a] + gifts:
+        for copy in [give_leaf] + give_a + gifts:
             copy.wait_send()
         for r in range(2):
             for k in range(1, 4):
                 round_copy(r, k).wait_send()
         for u in range(1, UPL):
             upper_copy(u).wait_send()
+        for _, across in [leaf_columns(n) for n in range(4)] + [low_levels()]:
+            across.wait_recv()
 
     @pl.loop(0, part - 1)
     def _(t):
@@ -529,8 +622,6 @@
 
     for copy in pts_copies + pair_copies + direct + passed(0) + passed(1):
         copy.wait_send()
-    for copy in publish_leaf() + publish_local():
-        copy.wait()
 
 
 def write_out(a, b, c, e, out_a, out_b, out_c, out_e, buf_a, buf_b, buf_c, buf_e, in_sem, out_sem):
@@ -612,6 +703,8 @@
             pltpu.VMEM((UPL - 1, 2, rank, total), F32),
             pltpu.VMEM((total, 2 * rank), F32),
             pltpu.VMEM((2, rank, size), F32),
+            pltpu.VMEM((4, 2, 4, rank, size), F32),
+            pltpu.VMEM((2, group - 4, rank, 2 * rank), F32),
             pltpu.VMEM((2, 6, rank, 2 * rank), F32),
             pltpu.VMEM((UPL, rank, 2 * rank), F32),
             pltpu.VMEM((1, columns, rank), F32),
@@ -624,10 +717,10 @@
             dma((2, part)),
             dma((6 + UPL,)),
             dma((6 + UPL,)),
-            dma((6 + UPL,)),
-            dma((6 + UPL,)),
-            dma((group + 5,)),
-            dma((group + 5,)),
+            dma((12 + UPL,)),
+            dma((12 + UPL,)),
+            dma((28,)),
+            dma((28,)),
             dma((5 + UPL,)),
         ],
         compiler_params=pltpu.CompilerParams(

time: 65.1 us -> 64.6 us (level)
  no operation moved by 1% of the time
where the time goes in v4:
time: 64.6 us; the launch traced here: 64.5 us
  Pallas kernels  63.8 us (99%)
    pallas_call x1, Pallas kernels, on_device(): pl.pallas_call(functools.partial(body, leaf_n, vec_n, axes), out_shape=sh...  61.6 us
    pallas_call x1, Pallas kernels, on_device(): pl.pallas_call(write_out, out_shape=shapes, in_specs=[anywhere] * 4, out_...  2.26 us

profile of v4, /device:TPU:1, one launch (start us, length us, event | category | flops | bytes accessed | tf_op | source)
XLA Modules:
  0.0 64.5 jit_solution(3131825310156646554)
XLA Ops:
  0.6 61.6 %shard_map.120 = (f32[16,64,256]{2,1,0:T(8,128)}, f32[15,64,128]{2,1,0:T(8,128)}, f32[1,3,64,128]{3,2,1,0:T(8,128)}, f32[1,16,64]{2,1,0:T(8,128)}) custom-call(bf16[3,16,256]{2,1,0:T(8,128)(2,1)} %bitcast.4, bf16[16,16,256]{2,1,0:T(8,128)(2,1)} %probe.1, s32[16,16]{1,0:T(8,128)} %nbr_in.1, s32[16,64]{1,0:T(8,128)} %leaf_piv.1, f32[16,64,64]{2,1,0:T(8,128)} %leaf_inv.1, ...), custom_call_target="tpu_custom_call" | custom-call | tf_op jit(solution)/shard_map/pallas_call | solution.py:682
  62.2 2.3 %shard_map.121 = (f32[16,64,256]{2,1,0:T(8,128)}, f32[15,64,128]{2,1,0:T(8,128)}, f32[1,3,64,128]{3,2,1,0:T(8,128)}, f32[1,16,64]{2,1,0:T(8,128)}) custom-call(f32[16,64,256]{2,1,0:T(8,128)} %get-tuple-element.12.a, f32[15,64,128]{2,1,0:T(8,128)} %get-tuple-element.13.b, f32[1,3,64,128]{3,2,1,0:T(8,128)} %get-tuple-element.14.c, ...), custom_call_target="tpu_custom_call" | custom-call | tf_op jit(solution)/shard_map/pallas_call | solution.py:740

commit v5 on v4

--- a/solution.py
+++ b/solution.py
@@ -140,7 +140,10 @@
     lead_row = d - core + 1
 
     barrier = pltpu.get_barrier_semaphore()
-    targets = [on_vec((v + t) % vec_n) for t in range(1, vec_n)]
+    targets = []
+    for t in range(1, 4):
+        row = 4 * ((y + t) % 4)
+        targets += [on_vec(u) for u in (4 * y + (x + t) % 4, row + x, row + 3 - x)]
     targets += [on_leaf(g) for g in (before, after, flip(d, 2), flip(d, 4))]
     targets += [
         {leaf_axis: mate, vec_axis: vec_of(half * part + (own + t) % part)}
@@ -360,26 +363,26 @@
     steps = (1, 3)
     order = (0, 3, 1, 2)
 
-    def full_x(way, o):
+    def full_x(way):
+        return same(16 + way, all_leaf.at[x, :, y], steps[way], 0)
+
+    def half_x(way):
+        source = (x + 4 - steps[way]) % 4
+        return same(18 + way, all_leaf.at[source, way, y], steps[way], 0)
+
+    def full_y(way, o):
         return same(
-            4 * way + o, all_leaf.at[x, :, (y + order[o]) % 4], steps[way], 0
-        )
-
-    def half_x(way, o):
-        source = (x + 4 - steps[way]) % 4
+            4 * way + o, all_leaf.at[(x + order[o]) % 4, :, y], 0, steps[way]
+        )
+
+    def half_y(way, o):
+        source = (y + 4 - steps[way]) % 4
         return same(
             8 + 4 * way + o,
-            all_leaf.at[source, way, (y + order[o]) % 4],
+            all_leaf.at[(x + order[o]) % 4, way, source],
+            0,
             steps[way],
-            0,
-        )
-
-    def full_y(way):
-        return same(16 + way, all_leaf.at[x, :, y], 0, steps[way])
-
-    def half_y(way):
-        source = (y + 4 - steps[way]) % 4
-        return same(18 + way, all_leaf.at[x, way, source], 0, steps[way])
+        )
 
     def local_rows(q, n):
         return pl.ds(2 * column(q), 2) if n == 0 else pl.ds(group // 2 + column(q), 1)
@@ -472,57 +475,50 @@
         last.start()
         give_leaf.wait_recv()
         for way in range(2):
-            full_y(way).start()
-        for way in range(2):
-            full_x(way, 0).start()
+            full_x(way).start()
+        for way in range(2):
+            full_y(way, 0).start()
         for came in range(2):
-            full_y(came).wait_recv()
-            half_y(came).start()
+            full_x(came).wait_recv()
+            half_x(came).start()
             for way in range(2):
-                full_x(way, 1 + came).start()
-        for way in range(2):
-            full_x(way, 0).wait_recv()
-            half_x(way, 0).start()
-        for way in range(2):
-            half_y(way).wait_recv()
-        for way in range(2):
-            full_x(way, 3).start()
-        for copy in leaf_columns(0):
-            copy.start()
-        for o in (1, 2):
-            for way in range(2):
-                full_x(way, o).wait_recv()
-                half_x(way, o).start()
+                full_y(way, 1 + came).start()
+        for way in range(2):
+            half_x(way).wait_recv()
+        for way in range(2):
+            full_y(way, 3).start()
+        for way in range(2):
+            full_y(way, 0).wait_recv()
+            half_y(way, 0).start()
         for copy in give_a:
             copy.wait_recv()
         for way in range(2):
             for n in range(2):
                 full_local(way, n).start()
-        for way in range(2):
-            full_x(way, 3).wait_recv()
-            half_x(way, 3).start()
-        for copy in leaf_columns(1) + leaf_columns(3):
-            copy.start()
+        for o in range(1, 4):
+            for way in range(2):
+                full_y(way, o).wait_recv()
+                half_y(way, o).start()
         for way in range(2):
             for n in range(2):
                 full_local(way, n).wait_recv()
                 half_local(way, n).start()
         for o in range(4):
             for way in range(2):
-                half_x(way, o).wait_recv()
-        for copy in leaf_columns(2):
-            copy.start()
+                half_y(way, o).wait_recv()
+            for copy in leaf_columns(order[o]):
+                copy.start()
         for way in range(2):
             for n in range(2):
                 half_local(way, n).wait_recv()
         for copy in low_levels():
             copy.start()
         for way in range(2):
-            full_y(way).wait_send()
-            half_y(way).wait_send()
+            full_x(way).wait_send()
+            half_x(way).wait_send()
             for o in range(4):
-                full_x(way, o).wait_send()
-                half_x(way, o).wait_send()
+                full_y(way, o).wait_send()
+                half_y(way, o).wait_send()
             for n in range(2):
                 full_local(way, n).wait_send()
                 half_local(way, n).wait_send()
@@ -551,13 +547,15 @@
             made = node((weights[g, 0, 0], weights[g, 0, 1]), z, jnp.transpose(z))
             leaf_map[g] = made[0]
             quad[0, pos, g] = up_of(*made)
+        give_leaf.start()
         for r in range(2):
             pos = w % 4 if r == 0 else quarter
             branch = pos // 2
             for k in (1, 3, 2):
                 round_copy(r, k).start()
-            for copy in (give_a if r else [give_leaf]):
-                copy.start()
+            if r == 1:
+                for copy in give_a:
+                    copy.start()
             for which, side in ((0, branch), (1, 1 - branch)):
                 for k in ((1,), (2, 3))[which]:
                     round_copy(r, k).wait_recv()

time: 64.6 us -> 59.4 us (0.920)
  Pallas kernels: 63.8 us -> 58.6 us
    pallas_call x1, Pallas kernels: 61.6 us -> 56.4 us  [on_device(): pl.pallas_call(functools.partial(body, leaf_n, vec_n, axes), out_shape=sh...]
where the time goes in v5:
time: 59.4 us; the launch traced here: 59.3 us
  Pallas kernels  58.6 us (99%)
  between operations  0.64 us (1%)
    pallas_call x1, Pallas kernels, on_device(): pl.pallas_call(functools.partial(body, leaf_n, vec_n, axes), out_shape=sh...  56.4 us
    pallas_call x1, Pallas kernels, on_device(): pl.pallas_call(write_out, out_shape=shapes, in_specs=[anywhere] * 4, out_...  2.26 us

profile of v5, /device:TPU:1, one launch (start us, length us, event | category | flops | bytes accessed | tf_op | source)
XLA Modules:
  0.0 59.3 jit_solution(14577888435883701774)
XLA Ops:
  0.6 56.4 %shard_map.120 = (f32[16,64,256]{2,1,0:T(8,128)}, f32[15,64,128]{2,1,0:T(8,128)}, f32[1,3,64,128]{3,2,1,0:T(8,128)}, f32[1,16,64]{2,1,0:T(8,128)}) custom-call(bf16[3,16,256]{2,1,0:T(8,128)(2,1)} %bitcast.4, bf16[16,16,256]{2,1,0:T(8,128)(2,1)} %probe.1, s32[16,16]{1,0:T(8,128)} %nbr_in.1, s32[16,64]{1,0:T(8,128)} %leaf_piv.1, f32[16,64,64]{2,1,0:T(8,128)} %leaf_inv.1, ...), custom_call_target="tpu_custom_call" | custom-call | tf_op jit(solution)/shard_map/pallas_call | solution.py:680
  57.0 2.3 %shard_map.121 = (f32[16,64,256]{2,1,0:T(8,128)}, f32[15,64,128]{2,1,0:T(8,128)}, f32[1,3,64,128]{3,2,1,0:T(8,128)}, f32[1,16,64]{2,1,0:T(8,128)}) custom-call(f32[16,64,256]{2,1,0:T(8,128)} %get-tuple-element.12.a, f32[15,64,128]{2,1,0:T(8,128)} %get-tuple-element.13.b, f32[1,3,64,128]{3,2,1,0:T(8,128)} %get-tuple-element.14.c, ...), custom_call_target="tpu_custom_call" | custom-call | tf_op jit(solution)/shard_map/pallas_call | solution.py:738

commit v6 on v5

--- a/solution.py
+++ b/solution.py
@@ -285,6 +285,13 @@
     def _():
         give_weights.start()
 
+    def tile(place, cluster):
+        return lax.rsqrt(mm(far[place], near[cluster])).astype(BF16)
+
+    for c in range(part):
+        cluster = half * part + c
+        tiles[c, :points, :] = tile(group + cluster, cluster)
+
     pts_copies[0].wait_recv()
     features(0)
     pts_copies[1].wait_recv()
@@ -299,12 +306,9 @@
     @pl.loop(0, part)
     def _(c):
         cluster = half * part + c
-        near_c = near[cluster]
-        for k in range(slots):
+        for k in range(1, slots):
             place, _ = place_of(cluster, k)
-            tiles[c, k * points : (k + 1) * points, :] = lax.rsqrt(
-                mm(far[place], near_c)
-            ).astype(BF16)
+            tiles[c, k * points : (k + 1) * points, :] = tile(place, cluster)
         for piece in range(2):
 
             @pl.when(c == 2 * piece)
@@ -452,20 +456,25 @@
             on_leaf(flip(d, 1 << u)),
         )
 
-    def node(scattered, z, zt):
-        size = zt.shape[0]
-        z_parts, zt_parts = split(z), split(zt)
-        mean_sq = jnp.sum(z * z) / (size * total) + EPSILON
-        gram = split(mm3(zt_parts, z_parts))
-        interp = mm3(scattered, gram) / (total * mean_sq)
-        return interp, mean_sq, zt_parts
-
-    def up_of(interp, mean_sq, zt_parts):
-        return mm3(split(interp), zt_parts) * lax.rsqrt(mean_sq)
+    def nodes(items):
+        parts = [split(zt) for _, zt in items]
+        mean_sq = [
+            jnp.sum(zt * zt) / (zt.shape[0] * total) + EPSILON for _, zt in items
+        ]
+        grams = [split(mm3(p, p, NT)) for p in parts]
+        return [
+            (mm3(scattered, gram) / (total * m), m, p)
+            for (scattered, _), gram, m, p in zip(items, grams, mean_sq, parts)
+        ]
+
+    def ups(made):
+        interps = [split(interp) for interp, _, _ in made]
+        return [
+            mm3(interp, p) * lax.rsqrt(m) for interp, (_, m, p) in zip(interps, made)
+        ]
 
     def join(left, right):
-        zt = jnp.concatenate([left, right], axis=0)
-        return jnp.transpose(zt), zt
+        return jnp.concatenate([left, right], axis=0)
 
     def local_weights(g, n):
         return weights[g, n, 0, :, : 2 * rank], weights[g, n, 1, :, : 2 * rank]
@@ -542,11 +551,16 @@
 
         last.wait_recv()
         pos = w % 4
+        made = nodes(
+            [
+                ((weights[g, 0, 0], weights[g, 0, 1]), jnp.transpose(z_ref[g]))
+                for g in range(2)
+            ]
+        )
+        raised = ups(made)
         for g in range(2):
-            z = z_ref[g]
-            made = node((weights[g, 0, 0], weights[g, 0, 1]), z, jnp.transpose(z))
-            leaf_map[g] = made[0]
-            quad[0, pos, g] = up_of(*made)
+            leaf_map[g] = made[g][0]
+            quad[0, pos, g] = raised[g]
         give_leaf.start()
         for r in range(2):
             pos = w % 4 if r == 0 else quarter
@@ -559,31 +573,43 @@
             for which, side in ((0, branch), (1, 1 - branch)):
                 for k in ((1,), (2, 3))[which]:
                     round_copy(r, k).wait_recv()
+                made = nodes(
+                    [
+                        (
+                            local_weights(g, 1 + 3 * r + side),
+                            join(quad[r, 2 * side, g], quad[r, 2 * side + 1, g]),
+                        )
+                        for g in range(2)
+                    ]
+                )
+                raised = ups(made)
                 for g in range(2):
-                    z, zt = join(quad[r, 2 * side, g], quad[r, 2 * side + 1, g])
-                    made = node(local_weights(g, 1 + 3 * r + side), z, zt)
-                    maps[g, 3 * r + side] = made[0]
-                    twin[r, side, g] = up_of(*made)
+                    maps[g, 3 * r + side] = made[g][0]
+                    twin[r, side, g] = raised[g]
+            made = nodes(
+                [
+                    (local_weights(g, 3 + 3 * r), join(twin[r, 0, g], twin[r, 1, g]))
+                    for g in range(2)
+                ]
+            )
+            raised = ups(made)
             for g in range(2):
-                z, zt = join(twin[r, 0, g], twin[r, 1, g])
-                made = node(local_weights(g, 3 + 3 * r), z, zt)
-                maps[g, 3 * r + 2] = made[0]
+                maps[g, 3 * r + 2] = made[g][0]
                 if r == 0:
-                    quad[1, quarter, g] = up_of(*made)
-                else:
-                    twin[2, 0, g] = up_of(*made)
+                    quad[1, quarter, g] = raised[g]
         give_b.start()
         own_b = pltpu.make_async_copy(
             maps.at[1, pl.ds(3, 3)], out_local.at[top_rows], out_sem.at[0]
         )
         own_b.start()
-        z, zt = join(twin[2, 0, 0], twin[2, 0, 1])
+        zt = join(*raised)
         own_upper = []
         for u in range(UPL):
-            made = node((upper_weights[u, 0], upper_weights[u, 1]), z, zt)
-            upper_maps[u] = made[0]
+            made = nodes([((upper_weights[u, 0], upper_weights[u, 1]), zt)])
+            interp, mean_sq, _ = made[0]
+            upper_maps[u] = interp
             if u + 1 < UPL:
-                joined[u, (d // (2 << u)) % 2] = up_of(*made)
+                joined[u, (d // (2 << u)) % 2] = ups(made)[0]
                 upper_copy(u + 1).start()
             give_upper[u].start()
             own_upper.append(
@@ -594,11 +620,11 @@
             own_upper[-1].start()
             if u + 1 < UPL:
                 upper_copy(u + 1).wait_recv()
-                z, zt = join(joined[u, 0], joined[u, 1])
+                zt = join(joined[u, 0], joined[u, 1])
             else:
-                z_top[...] = z
+                z_top[...] = jnp.transpose(zt)
                 kept = z_top[pl.ds(pl.multiple_of(v * columns, columns), columns), :]
-                top_ref[0] = mm3(split(kept), split(made[0]), NT) * lax.rsqrt(made[1])
+                top_ref[0] = mm3(split(kept), split(interp), NT) * lax.rsqrt(mean_sq)
         give_top.start()
         own_top = pltpu.make_async_copy(top_ref, out_top, out_sem.at[1 + UPL])
         own_top.start()
@@ -697,7 +723,7 @@
             pltpu.VMEM((part, 2 * columns, size), F32),
             pltpu.VMEM((2, total, size), F32),
             pltpu.VMEM((2, 4, 2, rank, total), F32),
-            pltpu.VMEM((3, 2, 2, rank, total), F32),
+            pltpu.VMEM((2, 2, 2, rank, total), F32),
             pltpu.VMEM((UPL - 1, 2, rank, total), F32),
             pltpu.VMEM((total, 2 * rank), F32),
             pltpu.VMEM((2, rank, size), F32),

time: 59.4 us -> 59.5 us (level)
  no operation moved by 1% of the time
where the time goes in v6:
time: 59.5 us; the launch traced here: 59.4 us
  Pallas kernels  58.7 us (99%)
  between operations  0.64 us (1%)
    pallas_call x1, Pallas kernels, on_device(): pl.pallas_call(functools.partial(body, leaf_n, vec_n, axes), out_shape=sh...  56.5 us
    pallas_call x1, Pallas kernels, on_device(): pl.pallas_call(write_out, out_shape=shapes, in_specs=[anywhere] * 4, out_...  2.26 us

profile of v6, /device:TPU:1, one launch (start us, length us, event | category | flops | bytes accessed | tf_op | source)
XLA Modules:
  0.0 59.4 jit_solution(11546791719492894066)
XLA Ops:
  0.6 56.5 %shard_map.120 = (f32[16,64,256]{2,1,0:T(8,128)}, f32[15,64,128]{2,1,0:T(8,128)}, f32[1,3,64,128]{3,2,1,0:T(8,128)}, f32[1,16,64]{2,1,0:T(8,128)}) custom-call(bf16[3,16,256]{2,1,0:T(8,128)(2,1)} %bitcast.4, bf16[16,16,256]{2,1,0:T(8,128)(2,1)} %probe.1, s32[16,16]{1,0:T(8,128)} %nbr_in.1, s32[16,64]{1,0:T(8,128)} %leaf_piv.1, f32[16,64,64]{2,1,0:T(8,128)} %leaf_inv.1, ...), custom_call_target="tpu_custom_call" | custom-call | tf_op jit(solution)/shard_map/pallas_call | solution.py:706
  57.1 2.3 %shard_map.121 = (f32[16,64,256]{2,1,0:T(8,128)}, f32[15,64,128]{2,1,0:T(8,128)}, f32[1,3,64,128]{3,2,1,0:T(8,128)}, f32[1,16,64]{2,1,0:T(8,128)}) custom-call(f32[16,64,256]{2,1,0:T(8,128)} %get-tuple-element.12.a, f32[15,64,128]{2,1,0:T(8,128)} %get-tuple-element.13.b, f32[1,3,64,128]{3,2,1,0:T(8,128)} %get-tuple-element.14.c, ...), custom_call_target="tpu_custom_call" | custom-call | tf_op jit(solution)/shard_map/pallas_call | solution.py:764

commit v7 on v6

--- a/solution.py
+++ b/solution.py
@@ -367,12 +367,8 @@
     steps = (1, 3)
     order = (0, 3, 1, 2)
 
-    def full_x(way):
-        return same(16 + way, all_leaf.at[x, :, y], steps[way], 0)
-
-    def half_x(way):
-        source = (x + 4 - steps[way]) % 4
-        return same(18 + way, all_leaf.at[source, way, y], steps[way], 0)
+    def to_x(way):
+        return same(16 + way, all_leaf.at[x, :, y], (1, 3, 2)[way], 0)
 
     def full_y(way, o):
         return same(
@@ -483,19 +479,14 @@
     def _():
         last.start()
         give_leaf.wait_recv()
-        for way in range(2):
-            full_x(way).start()
+        for way in range(3):
+            to_x(way).start()
         for way in range(2):
             full_y(way, 0).start()
-        for came in range(2):
-            full_x(came).wait_recv()
-            half_x(came).start()
+        for came in range(3):
+            to_x(came).wait_recv()
             for way in range(2):
                 full_y(way, 1 + came).start()
-        for way in range(2):
-            half_x(way).wait_recv()
-        for way in range(2):
-            full_y(way, 3).start()
         for way in range(2):
             full_y(way, 0).wait_recv()
             half_y(way, 0).start()
@@ -522,9 +513,9 @@
                 half_local(way, n).wait_recv()
         for copy in low_levels():
             copy.start()
+        for way in range(3):
+            to_x(way).wait_send()
         for way in range(2):
-            full_x(way).wait_send()
-            half_x(way).wait_send()
             for o in range(4):
                 full_y(way, o).wait_send()
                 half_y(way, o).wait_send()
@@ -557,11 +548,12 @@
                 for g in range(2)
             ]
         )
+        for g in range(2):
+            leaf_map[g] = made[g][0]
+        give_leaf.start()
         raised = ups(made)
         for g in range(2):
-            leaf_map[g] = made[g][0]
             quad[0, pos, g] = raised[g]
-        give_leaf.start()
         for r in range(2):
             pos = w % 4 if r == 0 else quarter
             branch = pos // 2

time: 59.5 us -> 57.4 us (0.965)
  Pallas kernels: 58.7 us -> 56.6 us
    pallas_call x1, Pallas kernels: 56.5 us -> 54.3 us  [on_device(): pl.pallas_call(functools.partial(body, leaf_n, vec_n, axes), out_shape=sh...]
where the time goes in v7:
time: 57.4 us; the launch traced here: 57.2 us
  Pallas kernels  56.6 us (99%)
  between operations  0.64 us (1%)
    pallas_call x1, Pallas kernels, on_device(): pl.pallas_call(functools.partial(body, leaf_n, vec_n, axes), out_shape=sh...  54.3 us
    pallas_call x1, Pallas kernels, on_device(): pl.pallas_call(write_out, out_shape=shapes, in_specs=[anywhere] * 4, out_...  2.26 us

profile of v7, /device:TPU:1, one launch (start us, length us, event | category | flops | bytes accessed | tf_op | source)
XLA Modules:
  0.0 57.2 jit_solution(16516844215544530375)
XLA Ops:
  0.6 54.3 %shard_map.120 = (f32[16,64,256]{2,1,0:T(8,128)}, f32[15,64,128]{2,1,0:T(8,128)}, f32[1,3,64,128]{3,2,1,0:T(8,128)}, f32[1,16,64]{2,1,0:T(8,128)}) custom-call(bf16[3,16,256]{2,1,0:T(8,128)(2,1)} %bitcast.4, bf16[16,16,256]{2,1,0:T(8,128)(2,1)} %probe.1, s32[16,16]{1,0:T(8,128)} %nbr_in.1, s32[16,64]{1,0:T(8,128)} %leaf_piv.1, f32[16,64,64]{2,1,0:T(8,128)} %leaf_inv.1, ...), custom_call_target="tpu_custom_call" | custom-call | tf_op jit(solution)/shard_map/pallas_call | solution.py:698
  55.0 2.3 %shard_map.121 = (f32[16,64,256]{2,1,0:T(8,128)}, f32[15,64,128]{2,1,0:T(8,128)}, f32[1,3,64,128]{3,2,1,0:T(8,128)}, f32[1,16,64]{2,1,0:T(8,128)}) custom-call(f32[16,64,256]{2,1,0:T(8,128)} %get-tuple-element.12.a, f32[15,64,128]{2,1,0:T(8,128)} %get-tuple-element.13.b, f32[1,3,64,128]{3,2,1,0:T(8,128)} %get-tuple-element.14.c, ...), custom_call_target="tpu_custom_call" | custom-call | tf_op jit(solution)/shard_map/pallas_call | solution.py:756

commit v8 on v7

--- a/solution.py
+++ b/solution.py
@@ -375,6 +375,9 @@
             4 * way + o, all_leaf.at[(x + order[o]) % 4, :, y], 0, steps[way]
         )
 
+    def to_far():
+        return same(19, all_leaf.at[(x + order[3]) % 4, :, y], 0, 2)
+
     def half_y(way, o):
         source = (y + 4 - steps[way]) % 4
         return same(
@@ -487,6 +490,7 @@
             to_x(came).wait_recv()
             for way in range(2):
                 full_y(way, 1 + came).start()
+        to_far().start()
         for way in range(2):
             full_y(way, 0).wait_recv()
             half_y(way, 0).start()
@@ -498,14 +502,18 @@
         for o in range(1, 4):
             for way in range(2):
                 full_y(way, o).wait_recv()
-                half_y(way, o).start()
+                if o < 3:
+                    half_y(way, o).start()
         for way in range(2):
             for n in range(2):
                 full_local(way, n).wait_recv()
                 half_local(way, n).start()
         for o in range(4):
-            for way in range(2):
-                half_y(way, o).wait_recv()
+            if o < 3:
+                for way in range(2):
+                    half_y(way, o).wait_recv()
+            else:
+                to_far().wait_recv()
             for copy in leaf_columns(order[o]):
                 copy.start()
         for way in range(2):
@@ -515,10 +523,12 @@
             copy.start()
         for way in range(3):
             to_x(way).wait_send()
+        to_far().wait_send()
         for way in range(2):
             for o in range(4):
                 full_y(way, o).wait_send()
-                half_y(way, o).wait_send()
+                if o < 3:
+                    half_y(way, o).wait_send()
             for n in range(2):
                 full_local(way, n).wait_send()
                 half_local(way, n).wait_send()

time: 57.4 us -> 58 us (1.010)
  Pallas kernels: 56.6 us -> 57.2 us
    pallas_call x1, Pallas kernels: 54.3 us -> 54.9 us  [on_device(): pl.pallas_call(functools.partial(body, leaf_n, vec_n, axes), out_shape=sh...]
where the time goes in v8:
time: 58 us; the launch traced here: 57.8 us
  Pallas kernels  57.2 us (99%)
  between operations  0.64 us (1%)
    pallas_call x1, Pallas kernels, on_device(): pl.pallas_call(functools.partial(body, leaf_n, vec_n, axes), out_shape=sh...  54.9 us
    pallas_call x1, Pallas kernels, on_device(): pl.pallas_call(write_out, out_shape=shapes, in_specs=[anywhere] * 4, out_...  2.26 us

profile of v8, /device:TPU:1, one launch (start us, length us, event | category | flops | bytes accessed | tf_op | source)
XLA Modules:
  0.0 57.8 jit_solution(7252009443742589132)
XLA Ops:
  0.6 54.9 %shard_map.120 = (f32[16,64,256]{2,1,0:T(8,128)}, f32[15,64,128]{2,1,0:T(8,128)}, f32[1,3,64,128]{3,2,1,0:T(8,128)}, f32[1,16,64]{2,1,0:T(8,128)}) custom-call(bf16[3,16,256]{2,1,0:T(8,128)(2,1)} %bitcast.4, bf16[16,16,256]{2,1,0:T(8,128)(2,1)} %probe.1, s32[16,16]{1,0:T(8,128)} %nbr_in.1, s32[16,64]{1,0:T(8,128)} %leaf_piv.1, f32[16,64,64]{2,1,0:T(8,128)} %leaf_inv.1, ...), custom_call_target="tpu_custom_call" | custom-call | tf_op jit(solution)/shard_map/pallas_call | solution.py:708
  55.6 2.3 %shard_map.121 = (f32[16,64,256]{2,1,0:T(8,128)}, f32[15,64,128]{2,1,0:T(8,128)}, f32[1,3,64,128]{3,2,1,0:T(8,128)}, f32[1,16,64]{2,1,0:T(8,128)}) custom-call(f32[16,64,256]{2,1,0:T(8,128)} %get-tuple-element.12.a, f32[15,64,128]{2,1,0:T(8,128)} %get-tuple-element.13.b, f32[1,3,64,128]{3,2,1,0:T(8,128)} %get-tuple-element.14.c, ...), custom_call_target="tpu_custom_call" | custom-call | tf_op jit(solution)/shard_map/pallas_call | solution.py:766
